TPU v7x, 32 devices: a whole 2x2x4 slice. The times are simulated.
32 devices in a mesh: dp: 16 (over z, y, x), tp: 2 (over core).
Axes of the slice: x: 2, y: 2, z: 4, core: 2. Of those that a mesh axis runs over, the one named last changes fastest.
Arguments:
- tokens: bfloat16 [32768, 768], P(('dp', 'tp')), may hold values from -6 to 6
- cotangent: bfloat16 [32768, 768], P(('dp', 'tp')), may hold values from -6 to 6
- lengths: int32 [16, 8], P('dp'), may hold values from 0 to 2048, as said below
- qkv_weight: bfloat16 [768, 2304], P(('dp', 'tp')), may hold values from -0.21875 to 0.21875
- out_weight: bfloat16 [768, 768], P(('dp', 'tp')), may hold values from -0.21875 to 0.21875
- pre_gain: bfloat16 [768], P(('dp', 'tp')), may hold values from 0.25 to 1.75
- pre_shift: bfloat16 [768], P(('dp', 'tp')), may hold values from -2 to 2
- sub_gain: bfloat16 [768], P(('dp', 'tp')), may hold values from 0.25 to 1.75
- sub_shift: bfloat16 [768], P(('dp', 'tp')), may hold values from -2 to 2
- ffn_gain: bfloat16 [768], P(('dp', 'tp')), may hold values from 0.25 to 1.75
- ffn_shift: bfloat16 [768], P(('dp', 'tp')), may hold values from -2 to 2
- fc1_weight: bfloat16 [3072, 768], P(('dp', 'tp')), may hold values from -0.21875 to 0.21875
- mid_gain: bfloat16 [3072], P(('dp', 'tp')), may hold values from 0.25 to 1.75
- mid_shift: bfloat16 [3072], P(('dp', 'tp')), may hold values from -2 to 2
- fc2_weight: bfloat16 [3072, 768], P(('dp', 'tp')), may hold values from -0.109375 to 0.109375
Outputs:
- block_out: bfloat16 [32768, 768], P(('dp', 'tp'))
- grad_tokens: bfloat16 [32768, 768], P(('dp', 'tp'))
- grad_qkv: float32 [768, 2304], P(('dp', 'tp'))
- grad_out: float32 [768, 768], P(('dp', 'tp'))
- grad_pre_gain: float32 [768], P(('dp', 'tp'))
- grad_pre_shift: float32 [768], P(('dp', 'tp'))
- grad_sub_gain: float32 [768], P(('dp', 'tp'))
- grad_sub_shift: float32 [768], P(('dp', 'tp'))
- grad_ffn_gain: float32 [768], P(('dp', 'tp'))
- grad_ffn_shift: float32 [768], P(('dp', 'tp'))
- grad_fc1: float32 [3072, 768], P(('dp', 'tp'))
- grad_mid_gain: float32 [3072], P(('dp', 'tp'))
- grad_mid_shift: float32 [3072], P(('dp', 'tp'))
- grad_fc2: float32 [3072, 768], P(('dp', 'tp'))
Inputs may be any that keep to these rules, and one draw needn't show every extreme that they name: `lengths`: each row lists one chip's sequences in the order they are packed; a row sums to 2048. Half of the chips, drawn from the seed, hold sequences of fewer than 512 tokens in which every two slots (0 and 1, 2 and 3, ...) sum to 512; the other half hold one sequence of more than 1024 tokens in slot 0, the rest of the rows in slot 1 (possibly 0), and zeros in the remaining slots.
All inputs are finite; a program needn't handle non-finite values.
Results may differ from a plain program's by a relative error of at most 0.012.
Values may be sent and summed in bfloat16 or wider, within the bound.
A program may use at most 192 MiB of HBM per device.

v0:
```python
import jax
import jax.numpy as jnp
from jax import lax
from jax.sharding import PartitionSpec as P

HEAD_DIM = 64
FF = 3072


eps = 1e-05


def layer_norm(values, factor, offset):
    centre = values - jnp.mean(values, axis=-1, keepdims=True)
    spread = jnp.mean(centre * centre, axis=-1, keepdims=True)
    return centre * lax.rsqrt(spread + eps) * factor + offset


def gelu_exact(values):
    return jax.nn.gelu(values, approximate=False)


def document_ids(bounds, places):
    return jnp.sum((places[:, None] >= bounds[None, :]).astype(jnp.int32), axis=1, dtype=jnp.int32)


def masked_scores(query_rows, key_cols, query_doc, query_place, key_doc, key_place):
    row_count = query_rows.shape[0]
    query_heads = query_rows.reshape(row_count, 2, HEAD_DIM)
    key_heads = key_cols.reshape(key_cols.shape[0], 2, HEAD_DIM)
    scores = jnp.einsum(
        "qhd,khd->hqk", query_heads, key_heads, preferred_element_type=jnp.float32
    ) * HEAD_DIM ** (-0.5)
    allowed = (query_doc[:, None] == key_doc[None, :]) & (
        key_place[None, :] <= query_place[:, None]
    )
    return jnp.where(allowed[None], scores, -1e30)


def attend_forward(queries, chip_keys, chip_values, query_doc, query_place, key_doc, key_place):
    row_count, model_width = queries.shape
    pair_width = 2 * HEAD_DIM
    block_rows = min(512, row_count)
    block_count = row_count // block_rows
    loop_count = model_width // pair_width * block_count

    def forward_step(counter, state):
        mixed_all, log_sums = state
        column = counter // block_count * pair_width
        first_row = counter % block_count * block_rows
        query_rows = lax.dynamic_slice(queries, (first_row, column), (block_rows, pair_width))
        key_cols = lax.dynamic_slice_in_dim(chip_keys, column, pair_width, 1)
        value_cols = lax.dynamic_slice_in_dim(chip_values, column, pair_width, 1)
        scores = masked_scores(
            query_rows,
            key_cols,
            lax.dynamic_slice_in_dim(query_doc, first_row, block_rows),
            lax.dynamic_slice_in_dim(query_place, first_row, block_rows),
            key_doc,
            key_place,
        )
        row_top = jnp.max(scores, axis=2, keepdims=True)
        exponent = jnp.exp(scores - row_top)
        summed = jnp.sum(exponent, axis=2, keepdims=True)
        weights = (exponent / summed).astype(jnp.bfloat16)
        value_heads = value_cols.reshape(value_cols.shape[0], 2, HEAD_DIM)
        mixed = jnp.einsum(
            "hqk,khd->qhd", weights, value_heads, preferred_element_type=jnp.float32
        ).reshape(block_rows, pair_width)
        mixed_all = lax.dynamic_update_slice(mixed_all, mixed, (first_row, column))
        log_sums = lax.dynamic_update_slice(
            log_sums,
            (row_top + jnp.log(summed))[:, :, 0],
            (2 * (counter // block_count), first_row),
        )
        return (mixed_all, log_sums)

    head_count = model_width // HEAD_DIM
    initial = (
        jnp.zeros((row_count, model_width), jnp.float32),
        jnp.zeros((head_count, row_count), jnp.float32),
    )
    return lax.fori_loop(0, loop_count, forward_step, initial)


def attend_backward(
    queries,
    chip_keys,
    chip_values,
    grad_mixed,
    log_sums,
    query_doc,
    query_place,
    key_doc,
    key_place,
):
    row_count, model_width = queries.shape
    key_count = chip_keys.shape[0]
    pair_width = 2 * HEAD_DIM
    block_rows = min(512, row_count)
    block_count = row_count // block_rows
    loop_count = model_width // pair_width * block_count
    factor = HEAD_DIM ** (-0.5)

    def backward_step(counter, state):
        grad_query, grad_key, grad_value = state
        column = counter // block_count * pair_width
        first_row = counter % block_count * block_rows
        query_rows = lax.dynamic_slice(queries, (first_row, column), (block_rows, pair_width))
        key_cols = lax.dynamic_slice_in_dim(chip_keys, column, pair_width, 1)
        value_cols = lax.dynamic_slice_in_dim(chip_values, column, pair_width, 1)
        scores = masked_scores(
            query_rows,
            key_cols,
            lax.dynamic_slice_in_dim(query_doc, first_row, block_rows),
            lax.dynamic_slice_in_dim(query_place, first_row, block_rows),
            key_doc,
            key_place,
        )
        lse_rows = lax.dynamic_slice(
            log_sums, (2 * (counter // block_count), first_row), (2, block_rows)
        )
        probs = jnp.exp(scores - lse_rows[:, :, None])
        grad_rows = lax.dynamic_slice(
            grad_mixed, (first_row, column), (block_rows, pair_width)
        ).reshape(block_rows, 2, HEAD_DIM)
        query_heads = query_rows.reshape(block_rows, 2, HEAD_DIM)
        key_heads = key_cols.reshape(key_count, 2, HEAD_DIM)
        value_heads = value_cols.reshape(key_count, 2, HEAD_DIM)
        grad_probs = jnp.einsum(
            "qhd,khd->hqk", grad_rows, value_heads, preferred_element_type=jnp.float32
        )
        inner = jnp.sum(grad_probs * probs, axis=2, keepdims=True)
        grad_scores = (probs * (grad_probs - inner)).astype(jnp.bfloat16)
        query_part = (
            jnp.einsum(
                "hqk,khd->qhd", grad_scores, key_heads, preferred_element_type=jnp.float32
            ).reshape(block_rows, pair_width)
            * factor
        )
        key_part = (
            jnp.einsum(
                "hqk,qhd->khd", grad_scores, query_heads, preferred_element_type=jnp.float32
            ).reshape(key_count, pair_width)
            * factor
        )
        value_part = jnp.einsum(
            "hqk,qhd->khd",
            probs.astype(jnp.bfloat16),
            grad_rows,
            preferred_element_type=jnp.float32,
        ).reshape(key_count, pair_width)
        grad_query = lax.dynamic_update_slice(grad_query, query_part, (first_row, column))
        grad_key = lax.dynamic_update_slice(
            grad_key,
            lax.dynamic_slice_in_dim(grad_key, column, pair_width, 1) + key_part,
            (0, column),
        )
        grad_value = lax.dynamic_update_slice(
            grad_value,
            lax.dynamic_slice_in_dim(grad_value, column, pair_width, 1) + value_part,
            (0, column),
        )
        return (grad_query, grad_key, grad_value)

    initial = (
        jnp.zeros((row_count, model_width), jnp.float32),
        jnp.zeros((key_count, model_width), jnp.float32),
        jnp.zeros((key_count, model_width), jnp.float32),
    )
    return lax.fori_loop(0, loop_count, backward_step, initial)


def local(
    tokens,
    cotangent,
    lengths,
    qkv_weight,
    out_weight,
    pre_gain,
    pre_shift,
    sub_gain,
    sub_shift,
    ffn_gain,
    ffn_shift,
    fc1_weight,
    mid_gain,
    mid_shift,
    fc2_weight,
):
    row_count, model_width = tokens.shape
    group_size = lax.axis_size("tp")
    first_place = lax.axis_index("tp") * row_count
    attention_own = (
        qkv_weight,
        out_weight,
        pre_gain,
        pre_shift,
        sub_gain,
        sub_shift,
        ffn_gain,
        ffn_shift,
    )
    hidden_own = (fc1_weight, mid_gain, mid_shift, fc2_weight)
    attention_set = (
        lax.all_gather(attention_own[0], ("dp", "tp"), axis=0, tiled=True),
        lax.all_gather(attention_own[1], ("dp", "tp"), axis=0, tiled=True),
        lax.all_gather(attention_own[2], ("dp", "tp"), axis=0, tiled=True),
        lax.all_gather(attention_own[3], ("dp", "tp"), axis=0, tiled=True),
        lax.all_gather(attention_own[4], ("dp", "tp"), axis=0, tiled=True),
        lax.all_gather(attention_own[5], ("dp", "tp"), axis=0, tiled=True),
        lax.all_gather(attention_own[6], ("dp", "tp"), axis=0, tiled=True),
        lax.all_gather(attention_own[7], ("dp", "tp"), axis=0, tiled=True),
    )
    hidden_set = (
        lax.all_gather(hidden_own[0], "dp", axis=0, tiled=True),
        lax.all_gather(hidden_own[1], "dp", axis=0, tiled=True),
        lax.all_gather(hidden_own[2], "dp", axis=0, tiled=True),
        lax.all_gather(hidden_own[3], "dp", axis=0, tiled=True),
    )
    bounds = jnp.cumsum(lengths[0], dtype=jnp.int32)
    key_place = jnp.arange(group_size * row_count, dtype=jnp.int32)
    query_place = first_place + jnp.arange(row_count, dtype=jnp.int32)
    key_doc = document_ids(bounds, key_place)
    query_doc = document_ids(bounds, query_place)
    inputs = tokens.astype(jnp.float32)
    normed_full, pre_back = jax.vjp(
        layer_norm,
        inputs,
        attention_set[2].astype(jnp.float32),
        attention_set[3].astype(jnp.float32),
    )
    normed = normed_full.astype(jnp.bfloat16)
    projected = jnp.dot(normed, attention_set[0], preferred_element_type=jnp.float32)
    queries = projected[:, :model_width].astype(jnp.bfloat16)
    keys_own = projected[:, model_width : 2 * model_width].astype(jnp.bfloat16)
    values_own = projected[:, 2 * model_width :].astype(jnp.bfloat16)
    chip_keys, chip_values = (
        lax.all_gather(keys_own, "tp", axis=0, tiled=True),
        lax.all_gather(values_own, "tp", axis=0, tiled=True),
    )
    attended, log_sums = attend_forward(
        queries, chip_keys, chip_values, query_doc, query_place, key_doc, key_place
    )
    sub_full, sub_back = jax.vjp(
        layer_norm,
        attended,
        attention_set[4].astype(jnp.float32),
        attention_set[5].astype(jnp.float32),
    )
    sub_normed = sub_full.astype(jnp.bfloat16)
    middle = inputs + jnp.dot(sub_normed, attention_set[1], preferred_element_type=jnp.float32)
    ffn_full, ffn_back = jax.vjp(
        layer_norm,
        middle,
        attention_set[6].astype(jnp.float32),
        attention_set[7].astype(jnp.float32),
    )
    ffn_normed = ffn_full.astype(jnp.bfloat16)
    chip_rows = lax.all_gather(ffn_normed, "tp", axis=0, tiled=True)
    pre_act = lax.dot_general(
        chip_rows, hidden_set[0], (((1,), (1,)), ((), ())), preferred_element_type=jnp.float32
    )
    activated, gelu_back = jax.vjp(gelu_exact, pre_act)
    first_sum, second_sum = lax.psum(
        (jnp.sum(activated, axis=1), jnp.sum(activated * activated, axis=1)), "tp"
    )
    row_mean = first_sum / FF
    inverse = lax.rsqrt(second_sum / FF - row_mean * row_mean + eps)
    centred = (activated - row_mean[:, None]) * inverse[:, None]
    mid_out = (
        centred * hidden_set[1].astype(jnp.float32) + hidden_set[2].astype(jnp.float32)
    ).astype(jnp.bfloat16)
    fc2_rows = hidden_set[3]
    ffn_out = lax.psum_scatter(
        jnp.dot(mid_out, fc2_rows, preferred_element_type=jnp.float32).astype(jnp.bfloat16),
        "tp",
        scatter_dimension=0,
        tiled=True,
    ).astype(jnp.float32)
    block_out = (middle + ffn_out).astype(jnp.bfloat16)
    attention_set = (
        lax.all_gather(attention_own[0], ("dp", "tp"), axis=0, tiled=True),
        lax.all_gather(attention_own[1], ("dp", "tp"), axis=0, tiled=True),
        lax.all_gather(attention_own[2], ("dp", "tp"), axis=0, tiled=True),
        lax.all_gather(attention_own[3], ("dp", "tp"), axis=0, tiled=True),
        lax.all_gather(attention_own[4], ("dp", "tp"), axis=0, tiled=True),
        lax.all_gather(attention_own[5], ("dp", "tp"), axis=0, tiled=True),
        lax.all_gather(attention_own[6], ("dp", "tp"), axis=0, tiled=True),
        lax.all_gather(attention_own[7], ("dp", "tp"), axis=0, tiled=True),
    )
    hidden_set = (
        lax.all_gather(hidden_own[0], "dp", axis=0, tiled=True),
        lax.all_gather(hidden_own[1], "dp", axis=0, tiled=True),
        lax.all_gather(hidden_own[2], "dp", axis=0, tiled=True),
        lax.all_gather(hidden_own[3], "dp", axis=0, tiled=True),
    )
    fc1_back = hidden_set[0]
    fc2_back = hidden_set[3]
    shard_rows = lax.all_gather(cotangent, "tp", axis=0, tiled=True)
    weight_sum = lax.dot_general(
        mid_out, shard_rows, (((0,), (0,)), ((), ())), preferred_element_type=jnp.float32
    )
    back_rows = lax.dot_general(
        shard_rows, fc2_back, (((1,), (1,)), ((), ())), preferred_element_type=jnp.float32
    )
    mid_gain_grad = jnp.sum(back_rows * centred, axis=0)
    mid_shift_grad = jnp.sum(back_rows, axis=0)
    scaled = back_rows * hidden_set[1].astype(jnp.float32)
    sum_plain, sum_cross = lax.psum(
        (jnp.sum(scaled, axis=1), jnp.sum(scaled * centred, axis=1)), "tp"
    )
    grad_act = inverse[:, None] * (
        scaled - sum_plain[:, None] / FF - centred * (sum_cross[:, None] / FF)
    )
    grad_pre = gelu_back(grad_act)[0].astype(jnp.bfloat16)
    fc1_grad = lax.dot_general(
        grad_pre, chip_rows, (((0,), (0,)), ((), ())), preferred_element_type=jnp.float32
    )
    grad_normed = lax.psum_scatter(
        jnp.dot(grad_pre, fc1_back, preferred_element_type=jnp.float32),
        "tp",
        scatter_dimension=0,
        tiled=True,
    )
    grad_from_ffn, ffn_gain_grad, ffn_shift_grad = ffn_back(grad_normed)
    grad_middle = cotangent.astype(jnp.float32) + grad_from_ffn
    grad_branch = grad_middle.astype(jnp.bfloat16)
    out_grad = lax.dot_general(
        sub_normed, grad_branch, (((0,), (0,)), ((), ())), preferred_element_type=jnp.float32
    )
    grad_sub = lax.dot_general(
        grad_branch, attention_set[1], (((1,), (1,)), ((), ())), preferred_element_type=jnp.float32
    )
    grad_attended, sub_gain_grad, sub_shift_grad = sub_back(grad_sub)
    grad_query, key_part, value_part = attend_backward(
        queries,
        chip_keys,
        chip_values,
        grad_attended.astype(jnp.bfloat16),
        log_sums,
        query_doc,
        query_place,
        key_doc,
        key_place,
    )
    grad_key, grad_value = (
        lax.psum_scatter(
            key_part.astype(jnp.bfloat16), "tp", scatter_dimension=0, tiled=True
        ).astype(jnp.float32),
        lax.psum_scatter(
            value_part.astype(jnp.bfloat16), "tp", scatter_dimension=0, tiled=True
        ).astype(jnp.float32),
    )
    grad_projected = jnp.concatenate([grad_query, grad_key, grad_value], axis=1).astype(
        jnp.bfloat16
    )
    qkv_grad = lax.dot_general(
        normed, grad_projected, (((0,), (0,)), ((), ())), preferred_element_type=jnp.float32
    )
    grad_normed_in = lax.dot_general(
        grad_projected,
        attention_set[0],
        (((1,), (1,)), ((), ())),
        preferred_element_type=jnp.float32,
    )
    grad_inputs, pre_gain_grad, pre_shift_grad = pre_back(grad_normed_in)
    grad_tokens = (grad_middle + grad_inputs).astype(jnp.bfloat16)
    summed_attention = (
        lax.psum_scatter(qkv_grad, ("dp", "tp"), scatter_dimension=0, tiled=True),
        lax.psum_scatter(out_grad, ("dp", "tp"), scatter_dimension=0, tiled=True),
        lax.psum_scatter(pre_gain_grad, ("dp", "tp"), scatter_dimension=0, tiled=True),
        lax.psum_scatter(pre_shift_grad, ("dp", "tp"), scatter_dimension=0, tiled=True),
        lax.psum_scatter(sub_gain_grad, ("dp", "tp"), scatter_dimension=0, tiled=True),
        lax.psum_scatter(sub_shift_grad, ("dp", "tp"), scatter_dimension=0, tiled=True),
        lax.psum_scatter(ffn_gain_grad, ("dp", "tp"), scatter_dimension=0, tiled=True),
        lax.psum_scatter(ffn_shift_grad, ("dp", "tp"), scatter_dimension=0, tiled=True),
    )
    summed_hidden = (
        lax.psum_scatter(fc1_grad, "dp", scatter_dimension=0, tiled=True),
        lax.psum_scatter(mid_gain_grad, "dp", scatter_dimension=0, tiled=True),
        lax.psum_scatter(mid_shift_grad, "dp", scatter_dimension=0, tiled=True),
        lax.psum_scatter(weight_sum, "dp", scatter_dimension=0, tiled=True),
    )
    return (
        block_out,
        grad_tokens,
        summed_attention[0],
        summed_attention[1],
        summed_attention[2],
        summed_attention[3],
        summed_attention[4],
        summed_attention[5],
        summed_attention[6],
        summed_attention[7],
        summed_hidden[0],
        summed_hidden[1],
        summed_hidden[2],
        summed_hidden[3],
    )


def solution(mesh):
    placed = (
        P(("dp", "tp"), None),
        P(("dp", "tp"), None),
        P("dp", None),
        P(("dp", "tp"), None),
        P(("dp", "tp"), None),
        P(("dp", "tp")),
        P(("dp", "tp")),
        P(("dp", "tp")),
        P(("dp", "tp")),
        P(("dp", "tp")),
        P(("dp", "tp")),
        P(("dp", "tp"), None),
        P(("dp", "tp")),
        P(("dp", "tp")),
        P(("dp", "tp"), None),
    )
    return jax.shard_map(
        local,
        mesh=mesh,
        in_specs=placed,
        out_specs=(
            P(("dp", "tp"), None),
            P(("dp", "tp"), None),
            P(("dp", "tp"), None),
            P(("dp", "tp"), None),
            P(("dp", "tp")),
            P(("dp", "tp")),
            P(("dp", "tp")),
            P(("dp", "tp")),
            P(("dp", "tp")),
            P(("dp", "tp")),
            P(("dp", "tp"), None),
            P(("dp", "tp")),
            P(("dp", "tp")),
            P(("dp", "tp"), None),
        ),
        check_vma=False,
    )
```

profile of v0, /device:TPU:0, one launch (start us, length us, event | category | flops | bytes accessed | tf_op | source)
XLA Modules:
  0.0 1464.4 jit_solution(5095049290680361535)
XLA Ops:
  13.0 42.4 %all-reduce.20 = (bf16[768]{0:T(1024)(128)(2,1)S(1)}, bf16[768]{0:T(1024)(128)(2,1)S(1)}, bf16[768]{0:T(1024)(128)(2,1)S(1)}, bf16[768]{0:T(1024)(128)(2,1)S(1)}...) all-reduce(bf16[768]{0:T(1024)(128)(2,1)S(1)} %dynamic-update-slice, ...), channel_id=1, replica_groups=mesh['dp'=16,'tp'=2] {'dp','tp'}, use_global_device_ids=true, to_apply=%add.1 | all-reduce | flops 4608 | bytes 18432
  58.7 15.1 %all-gather.9.cloned.1.call-done = bf16[768,2304]{1,0:T(8,128)(2,1)} async-done(((bf16[24,2304]{1,0:T(8,128)(2,1)}), bf16[768,2304]{1,0:T(8,128)(2,1)}) %all-gather.9.cloned.1.call-update) | async-done | bytes 3538960 | tf_op jit(solution)/shard_map/all_gather | solution.py:206
  73.8 6.4 convolution_convert_fusion
  98.0 10.7 all-gather.13.cloned.1.call-done
  115.6 228.8 %while.38 = (s32[]{:T(128)}, f32[1024,768]{0,1:T(8,128)}, f32[12,1024]{1,0:T(8,128)S(1)}, bf16[2048,768]{0,1:T(8,128)(2,1)}, s32[1024]{0:T(1024)S(1)}, /*index=5...) while((s32[]{:T(128)}, f32[1024,768]{0,1:T(8,128)}, ...), condition=%wide.region_8.9_spmd.clone, body=%wide.region_5.8_spmd.clone.sunk | while | flops 565181440 | bytes 67293664 | solution.py:83
  362.4 42.6 %all-reduce.21 = (bf16[1536]{0:T(1024)(128)(2,1)S(1)}, bf16[1536]{0:T(1024)(128)(2,1)S(1)}) all-reduce(bf16[1536]{0:T(1024)(128)(2,1)S(1)} %dynamic-update-slice.7, bf16[1536]{0:T(1024)(128)(2,1)S(1)} %dynamic-update-slice.6), channel_id=1, replica_groups=mesh['dp'=16,'tp'=2] {'dp'}, use_global_device_ids=true, to_apply=%add.7 | all-reduce | flops 3072 | bytes 12288
  405.1 10.6 fusion.54
  415.7 12.8 copy.72
  428.5 35.5 %fusion.46 = (f32[2048]{0:T(1024)S(1)}, f32[2048]{0:T(1024)S(1)}, f32[2048,1536]{0,1:T(8,128)}, f32[2048,1536]{0,1:T(8,128)}, f32[2048,1536]{0,1:T(8,128)}) fusion(bf16[1536,768]{1,0:T(8,128)(2,1)} %all-gather.19.cloned.1.call-done, bf16[2048,768]{0,1:T(8,128)(2,1)} %all-gather.17.cloned.1.call-done), kind=kOutput, calls=%fused_computation.118 | convolution fusion | flops 5042597888 | bytes 43270144 | tf_op jit(solution)/shard_map/dot_general | solution.py:261
  467.3 10.7 multiply_reduce_fusion.1
  481.8 21.8 %add_convert_fusion = (bf16[2048,1536]{0,1:T(8,128)(2,1)S(1)}, bf16[2048,1536]{0,1:T(8,128)(2,1)}) fusion(f32[2048,1536]{0,1:T(8,128)} %get-tuple-element.809, f32[2048,1536]{0,1:T(8,128)} %get-tuple-element.830, f32[2048,1536]{0,1:T(8,128)} %copy.72, f32[2048,1536]{0,1:T(8,128)} %get-tuple-element.808, f32[2048]{0:T(1024)S(1)} %get-tuple-element.836, ...), kind=kLoop, calls=%fused_computation.36 | loop fusion | flops 75497472 | bytes 62959616 | tf_op jit(solution)/shard_map/convert_element_type | solution.py:316
  506.3 7.4 fusion.56
  515.4 10.0 convolution_convert_fusion.1
  558.1 351.4 %while.39 = (s32[]{:T(128)}, bf16[1024,768]{0,1:T(8,128)(2,1)}, f32[2048,768]{0,1:T(8,128)}, f32[2048,768]{0,1:T(8,128)}, bf16[2048,768]{0,1:T(8,128)(2,1)}, /*i...) while((s32[]{:T(128)}, bf16[1024,768]{0,1:T(8,128)(2,1)}, ...), condition=%wide.region_29.30_spmd.clone, body=%wide.region_27.29_spmd.clone.sunk | while | flops 1377696768 | bytes 106086912 | solution.py:171
  803.7 5.6 multiply_reduce_fusion.12
  921.4 9.1 fusion.57
  932.5 8.5 fusion.58
  947.8 9.3 fusion.35
  957.9 77.9 %all-reduce.17 = (f32[1536]{0:T(1024)S(1)}, f32[1536]{0:T(1024)S(1)}) all-reduce(f32[1536]{0:T(1024)S(1)} %copy-done.44, f32[1536]{0:T(1024)S(1)} %copy-done.53), channel_id=15, replica_groups=mesh['dp'=16,'tp'=2] {'dp'}, use_global_device_ids=true, to_apply=%region_50.51.clone | all-reduce | flops 3072 | bytes 24576
  1038.5 9.1 fusion.53
  1055.4 37.8 %all-reduce.16 = (f32[768]{0:T(1024)S(1)}, f32[768]{0:T(1024)S(1)}, f32[768]{0:T(1024)S(1)}, f32[768]{0:T(1024)S(1)}, f32[768]{0:T(1024)S(1)}, /*index=5*/f32[768]{0:T(1024)S(1)}) all-reduce(f32[768]{0:T(1024)S(1)} %get-tuple-element.738, f32[768]{0:T(1024)S(1)} %get-tuple-element.832, ...), channel_id=8, replica_groups=mesh['dp'=16,'tp'=2] {'dp','tp'}, use_global_device_ids=true, to_apply=%region_37.38.clone | all-reduce | flops 4608 | bytes 36864
  1104.8 123.6 %reduce-scatter.23.cloned.1.call-done = f32[96,768]{1,0:T(8,128)} async-done(((f32[1536,768]{1,0:T(8,128)}), f32[96,768]{1,0:T(8,128)}) %reduce-scatter.23.cloned.1.call-update) | async-done | bytes 294928 | tf_op jit(solution)/shard_map/reduce_scatter | solution.py:383
  1228.5 103.9 %reduce-scatter.19.cloned.1.call-done = f32[24,768]{1,0:T(8,128)} async-done(((f32[768,768]{1,0:T(8,128)}), f32[24,768]{1,0:T(8,128)}) %reduce-scatter.19.cloned.1.call-update) | async-done | bytes 73744 | tf_op jit(solution)/shard_map/reduce_scatter | solution.py:371
  1332.4 125.3 %reduce-scatter.17.cloned.1.call-done = f32[24,2304]{1,0:T(8,128)} async-done(((f32[768,2304]{1,0:T(8,128)}), f32[24,2304]{1,0:T(8,128)}) %reduce-scatter.17.cloned.1.call-update) | async-done | bytes 221200 | tf_op jit(solution)/shard_map/reduce_scatter | solution.py:370
  (673 shorter events, 709.9 us)
Async XLA Ops:
  7.2 66.6 %all-gather.9.cloned.1.call-start = ((), (), s32[]{:S(2)}) async-start(), calls=%async_computation.8 | async-start | bytes 3649536 | tf_op jit(solution)/shard_map/all_gather | solution.py:206
  7.9 85.4 %all-gather.11.cloned.1.call-start = ((), (), s32[]{:S(2)}) async-start(), calls=%async_computation.9 | async-start | bytes 4718592 | tf_op jit(solution)/shard_map/all_gather | solution.py:240
  57.4 295.2 %copy-start.1 = (bf16[1024,768]{0,1:T(8,128)(2,1)}, bf16[1024,768]{0,1:T(8,128)(2,1)S(1)}, u32[]{:S(2)}) copy-start(bf16[1024,768]{0,1:T(8,128)(2,1)S(1)} %copy.65) | copy-start | bytes 4718596
  82.2 26.5 %all-gather.13.cloned.1.call-start = ((), (), s32[]{:S(2)}) async-start(), calls=%async_computation.10 | async-start | bytes 4718592 | tf_op jit(solution)/shard_map/all_gather | solution.py:239
  82.9 269.6 %all-gather.15.cloned.1.call-start = ((), (), s32[]{:S(2)}) async-start(), calls=%async_computation.11 | async-start | bytes 1216512 | tf_op jit(solution)/shard_map/all_gather | solution.py:207
  83.5 321.5 %all-gather.23.cloned.1.call-start = ((), (), s32[]{:S(2)}) async-start(), calls=%async_computation.16 | async-start | bytes 4718592 | tf_op jit(solution)/shard_map/all_gather | solution.py:300
  84.1 321.0 %all-gather.21.cloned.1.call-start = ((), (), s32[]{:S(2)}) async-start(), calls=%async_computation.14 | async-start | bytes 2506752 | tf_op jit(solution)/shard_map/all_gather | solution.py:219
  84.7 343.8 %all-gather.19.cloned.1.call-start = ((), (), s32[]{:S(2)}) async-start(), calls=%async_computation.13 | async-start | bytes 2506752 | tf_op jit(solution)/shard_map/all_gather | solution.py:216
  85.4 343.1 %all-gather.17.cloned.1.call-start = ((), (), s32[]{:S(2)}) async-start(), calls=%async_computation.12 | async-start | bytes 4718592 | tf_op jit(solution)/shard_map/all_gather | solution.py:260
  86.0 266.5 %copy-start.45 = (f32[768]{0:T(1024)}, f32[768]{0:T(1024)S(1)}, u32[]{:S(2)}) copy-start(f32[768]{0:T(1024)S(1)} %convert_element_type.118) | copy-start | bytes 9220
  86.1 266.5 %copy-start.56 = (f32[768]{0:T(1024)}, f32[768]{0:T(1024)S(1)}, u32[]{:S(2)}) copy-start(f32[768]{0:T(1024)S(1)} %convert_element_type.119) | copy-start | bytes 9220
  86.1 271.9 %copy-start.25 = (f32[768]{0:T(1024)}, f32[768]{0:T(1024)S(1)}, u32[]{:S(2)}) copy-start(f32[768]{0:T(1024)S(1)} %convert_element_type.121) | copy-start | bytes 9220
  360.6 169.2 %reduce-scatter.11.cloned.1.call-start = ((), (), s32[]{:S(2)}) async-start(), calls=%async_computation.17 | async-start | bytes 9437184 | tf_op jit(solution)/shard_map/reduce_scatter | solution.py:320
  481.8 24.5 %copy-start.64 = (bf16[1536,768]{1,0:T(8,128)(2,1)S(1)}, bf16[1536,768]{1,0:T(8,128)(2,1)}, u32[]{:S(2)}) copy-start(bf16[1536,768]{1,0:T(8,128)(2,1)} %all-gather.19.cloned.1.call-done) | copy-start | bytes 7077892
  513.7 24.9 %reduce-scatter.9.cloned.1.call-start = ((), (), s32[]{:S(2)}) async-start(), calls=%async_computation.15 | async-start | bytes 4718592 | tf_op jit(solution)/shard_map/reduce_scatter | solution.py:275
  525.4 422.3 %reduce-scatter.13.cloned.1.call-start = ((), (), s32[]{:S(2)}) async-start(), calls=%async_computation.18 | async-start | bytes 4718592 | tf_op jit(solution)/shard_map/reduce_scatter | solution.py:348
  914.5 33.2 %reduce-scatter.15.cloned.1.call-start = ((), (), s32[]{:S(2)}) async-start(), calls=%async_computation.19 | async-start | bytes 4718592 | tf_op jit(solution)/shard_map/reduce_scatter | solution.py:351
  919.6 185.3 %reduce-scatter.21.cloned.1.call-start = ((), (), s32[]{:S(2)}) async-start(), calls=%async_computation.22 | async-start | bytes 5013504 | tf_op jit(solution)/shard_map/reduce_scatter | solution.py:380
  930.6 297.9 %reduce-scatter.23.cloned.1.call-start = ((), (), s32[]{:S(2)}) async-start(), calls=%async_computation.23 | async-start | bytes 5013504 | tf_op jit(solution)/shard_map/reduce_scatter | solution.py:383
  941.1 391.3 %reduce-scatter.19.cloned.1.call-start = ((), (), s32[]{:S(2)}) async-start(), calls=%async_computation.21 | async-start | bytes 2433024 | tf_op jit(solution)/shard_map/reduce_scatter | solution.py:371
  947.6 510.1 %reduce-scatter.17.cloned.1.call-start = ((), (), s32[]{:S(2)}) async-start(), calls=%async_computation.20 | async-start | bytes 7299072 | tf_op jit(solution)/shard_map/reduce_scatter | solution.py:370
  957.1 79.9 %copy-start.10 = (bf16[1024,768]{0,1:T(8,128)(2,1)S(1)}, bf16[1024,768]{0,1:T(8,128)(2,1)}, u32[]{:S(2)}) copy-start(bf16[1024,768]{0,1:T(8,128)(2,1)} %get-tuple-element.823) | copy-start | bytes 4718596
  1053.8 42.8 %copy-start.9 = (bf16[1024,768]{0,1:T(8,128)(2,1)S(1)}, bf16[1024,768]{0,1:T(8,128)(2,1)}, u32[]{:S(2)}) copy-start(bf16[1024,768]{0,1:T(8,128)(2,1)} %copy.71) | copy-start | bytes 4718596
  1053.8 42.8 %copy-start.43 = (f32[1024]{0:T(1024)S(1)}, f32[1024]{0:T(1024)}, u32[]{:S(2)}) copy-start(f32[1024]{0:T(1024)} %copy-done.42) | copy-start | bytes 12292
  (96 other events, 411.1 us)
Sparse Core Ops, SparseCore 0:
  10.9 62.8 all-gather.8
  82.3 10.9 all-gather.10
  95.4 13.2 all-gather.12
  111.5 55.2 all-gather.14
  168.1 11.0 all-gather.22
  181.9 63.5 all-gather.20
  248.2 61.1 all-gather.18
  360.7 13.1 all-gather.16
  513.8 10.4 reduce-scatter.10
  526.5 12.0 reduce-scatter.8
  914.6 12.0 reduce-scatter.12
  928.9 12.0 reduce-scatter.14
  946.7 139.0 reduce-scatter.20
  1092.2 136.1 reduce-scatter.22
  1234.2 98.1 reduce-scatter.18
  1339.4 118.1 reduce-scatter.16
where the time goes:
time: 1470 us; the launch traced here: 1460 us
  waiting for transfers between devices  393 us (27%)
  matrix products  376 us (26%)
  local copies, waits for them, and re-layouts  268 us (18%)
  blocking collectives  208 us (14%)
  other arithmetic  199 us (14%)
  between operations  16.4 us (1%)
    unnamed x4, blocking collectives  201 us
    reduce_scatter x1, waiting for transfers between devices, local(): lax.psum_scatter(qkv_grad, ('dp', 'tp'), scatter_dimension=0, tiled=True)  125 us
    reduce_scatter x1, waiting for transfers between devices, local(): lax.psum_scatter(weight_sum, 'dp', scatter_dimension=0, tiled=True)  124 us
    reduce_scatter x1, waiting for transfers between devices, local(): lax.psum_scatter(out_grad, ('dp', 'tp'), scatter_dimension=0, tiled=True)  104 us
    dot_general x24, matrix products, masked_scores(): jnp.einsum('qhd,khd->hqk', query_heads, key_heads, preferred_element_type...  77.8 us
    dot_general x12, matrix products, backward_step(): jnp.einsum('qhd,khd->hqk', grad_rows, value_heads, preferred_element_type...  67.3 us
    dot_general x12, matrix products, forward_step(): jnp.einsum('hqk,khd->qhd', weights, value_heads, preferred_element_type=j...  56.8 us
    unnamed x168, local copies, waits for them, and re-layouts  45.5 us
  transfers between devices with their start and end apart: 16, of which 7 were waited for; matrix products, arithmetic and copies ran while one was open for 23% of the time, Pallas kernels for 0%

commit v1 on v0

v1 whole, which is shorter than its diff:
```python
import functools

import jax
import jax.numpy as jnp
from jax import lax
from jax.experimental import pallas as pl
from jax.experimental.pallas import tpu as pltpu
from jax.sharding import PartitionSpec as P

f32, bf16 = jnp.float32, jnp.bfloat16
EPS = 1e-5
BIG = 1e30


def nt(a, b):
    return lax.dot_general(a, b, (((1,), (1,)), ((), ())), preferred_element_type=f32)


def nn(a, b):
    return lax.dot_general(a, b, (((1,), (0,)), ((), ())), preferred_element_type=f32)


def tn(a, b):
    return lax.dot_general(a, b, (((0,), (0,)), ((), ())), preferred_element_type=f32)

def doc_features(len_ref, rows, fq, fk):
    lane = lax.broadcasted_iota(jnp.int32, (1, 128), 1)
    lo = jnp.zeros((1, 128), jnp.int32); hi = jnp.zeros((1, 128), jnp.int32)
    run = jnp.int32(0)
    for d in range(8):
        nxt = run + len_ref[0, d]
        lo = jnp.where(lane == d, run, lo); hi = jnp.where(lane == d, nxt, hi)
        run = nxt
    def body(r, _):
        place = lax.broadcasted_iota(jnp.int32, (256, 128), 0) + r * 256
        hit = (place >= lo) & (place < hi)
        sl = pl.ds(pl.multiple_of(r * 256, 256), 256)
        fq[sl, :] = jnp.where(hit, 1.0, 0.0).astype(bf16)
        fk[sl, :] = jnp.where(hit | (lane >= 8), 0.0, -BIG).astype(bf16)
        return 0
    lax.fori_loop(0, rows // 256, body, 0)

def fwd_t(len_ref, qkv, o_ref, lse_ref, fq, fk, q2, st_s, m_s, l_s, acc, *, B, pairs, variant):
    rows = qkv.shape[0]; nb = rows // B; W = pairs * 128
    doc_features(len_ref, rows, fq, fk)
    half = lax.broadcasted_iota(jnp.int32, (1, 128), 1) < 64
    causal = lax.broadcasted_iota(jnp.int32, (B, B), 0) <= lax.broadcasted_iota(jnp.int32, (B, B), 1)
    causal = jnp.concatenate([causal, causal], axis=1)
    for p in range(pairs):
        def qstep(i, _, p=p):
            qs = pl.ds(pl.multiple_of(i * B, B), B)
            q = qkv[qs, p * 128:(p + 1) * 128] * bf16(0.125)
            fqb = fq[qs, :]
            z = jnp.zeros_like(q)
            q2[...] = jnp.concatenate([
                jnp.concatenate([jnp.where(half, q, z), fqb], axis=1),
                jnp.concatenate([jnp.where(half, z, q), fqb], axis=1)], axis=0)
            def score(j):
                ks = pl.ds(pl.multiple_of(j * B, B), B)
                k2 = jnp.concatenate([qkv[ks, W + p * 128:W + (p + 1) * 128], fk[ks, :]], axis=1)
                return nt(k2, q2[...])
            def vblk(j):
                ks = pl.ds(pl.multiple_of(j * B, B), B)
                return qkv[ks, 2 * W + p * 128:2 * W + (p + 1) * 128]
            if variant == "online":
                def block(j, masked, first):
                    s = score(j)
                    if masked: s = jnp.where(causal, s, -BIG)
                    mx = jnp.max(s, axis=0, keepdims=True)
                    if first: mn = mx
                    else:
                        mo = m_s[...]
                        mn = jnp.maximum(mo, mx); al = jnp.exp(mo - mn)
                    e = jnp.exp(s - mn)
                    su = jnp.sum(e, axis=0, keepdims=True)
                    pv = tn(vblk(j), e.astype(bf16))
                    if first: l_s[...] = su; acc[...] = pv
                    else: l_s[...] = l_s[...] * al + su; acc[...] = acc[...] * al + pv
                    m_s[...] = mn
                block(i, True, True)
                def kstep(j, _):
                    block(j, False, False); return 0
                lax.fori_loop(0, i, kstep, 0)
                m = m_s[...]; l = l_s[...]
            else:
                def part(s): return jnp.max(s.reshape(B // 8, 8, 2 * B), axis=0)
                s = jnp.where(causal, score(i), -BIG)
                st_s[i] = s
                def pass1(j, m8):
                    s = score(j); st_s[j] = s
                    return jnp.maximum(m8, part(s))
                m8 = lax.fori_loop(0, i, pass1, part(s))
                m = jnp.max(m8, axis=0, keepdims=True)
                acc[...] = jnp.zeros_like(acc)
                def pass2(j, l8):
                    e = jnp.exp(st_s[j] - m)
                    acc[...] += tn(vblk(j), e.astype(bf16))
                    return l8 + jnp.sum(e.reshape(B // 8, 8, 2 * B), axis=0)
                l8 = lax.fori_loop(0, i + 1, pass2, jnp.zeros((8, 2 * B), f32))
                l = jnp.sum(l8, axis=0, keepdims=True)
            r = 1.0 / l
            a = acc[...] * r
            ot = jnp.concatenate([a[:64, :B], a[64:, B:]], axis=0)
            o_ref[qs, p * 128:(p + 1) * 128] = ot.T.astype(o_ref.dtype)
            lse = m + jnp.log(l)
            lse_ref[2 * p:2 * p + 1, qs] = lse[:, :B]
            lse_ref[2 * p + 1:2 * p + 2, qs] = lse[:, B:]
            return 0
        lax.fori_loop(0, nb, qstep, 0)

def attn_fwd(lengths, qkv, B=256, variant="online"):
    rows, w3 = qkv.shape; W = w3 // 3; pairs = W // 128; nb = rows // B
    return pl.pallas_call(functools.partial(fwd_t, B=B, pairs=pairs, variant=variant), name="attn_fwd",
        out_shape=(jax.ShapeDtypeStruct((rows, W), bf16), jax.ShapeDtypeStruct((8, rows), f32)),
        in_specs=[pl.BlockSpec(memory_space=pltpu.SMEM), pl.BlockSpec(memory_space=pltpu.VMEM)],
        out_specs=(pl.BlockSpec(memory_space=pltpu.VMEM),) * 2,
        scratch_shapes=[pltpu.VMEM((rows, 128), bf16), pltpu.VMEM((rows, 128), bf16), pltpu.VMEM((2 * B, 256), bf16),
                        pltpu.VMEM((nb if variant != "online" else 1, B, 2 * B), f32),
                        pltpu.VMEM((1, 2 * B), f32), pltpu.VMEM((1, 2 * B), f32), pltpu.VMEM((128, 2 * B), f32)],
        compiler_params=pltpu.CompilerParams(vmem_limit_bytes=56 << 20))(lengths, qkv)

def bwd_kernel(len_ref, qkv, do_ref, lse_ref, dl_ref, out, fq, fk, q2, do2, dq, dk, dv, *, B, pairs, mode):
    rows = qkv.shape[0]; nb = rows // B; W = pairs * 128
    doc_features(len_ref, rows, fq, fk)
    half = lax.broadcasted_iota(jnp.int32, (1, 128), 1) < 64
    causal = lax.broadcasted_iota(jnp.int32, (B, B), 0) <= lax.broadcasted_iota(jnp.int32, (B, B), 1)
    causal = jnp.concatenate([causal, causal], axis=1)
    for p in range(pairs):
        def prep(i, _, p=p):
            qs = pl.ds(pl.multiple_of(i * B, B), B)
            q = qkv[qs, p * 128:(p + 1) * 128] * bf16(0.125)
            d = do_ref[qs, p * 128:(p + 1) * 128]
            fqb = fq[qs, :]
            z = jnp.zeros_like(q)
            q2[i] = jnp.concatenate([
                jnp.concatenate([jnp.where(half, q, z), fqb], axis=1),
                jnp.concatenate([jnp.where(half, z, q), fqb], axis=1)], axis=0)
            do2[i] = jnp.concatenate([jnp.where(half, d, z), jnp.where(half, z, d)], axis=0)
            dq[i] = jnp.zeros(dq.shape[1:], f32)
            return 0
        lax.fori_loop(0, nb, prep, 0)
        def kstep(j, _, p=p):
            ks = pl.ds(pl.multiple_of(j * B, B), B)
            kt = qkv[ks, W + p * 128:W + (p + 1) * 128]
            v = qkv[ks, 2 * W + p * 128:2 * W + (p + 1) * 128]
            k2 = jnp.concatenate([kt, fk[ks, :]], axis=1)
            def block(i, masked, first):
                qs = pl.ds(pl.multiple_of(i * B, B), B)
                lse = jnp.concatenate([lse_ref[2 * p:2 * p + 1, qs], lse_ref[2 * p + 1:2 * p + 2, qs]], axis=1)
                dl = jnp.concatenate([dl_ref[2 * p:2 * p + 1, qs], dl_ref[2 * p + 1:2 * p + 2, qs]], axis=1)
                qq = q2[i]; dd = do2[i]
                st = nt(k2, qq)
                pt = jnp.exp(st - lse)
                if masked: pt = jnp.where(causal, pt, 0.0)
                dp = nt(v, dd)
                ds = (pt * (dp - dl)).astype(bf16)
                dvp = nn(pt.astype(bf16), dd)
                dkp = nn(ds, qq[:, :128])
                if first: dv[...] = dvp; dk[...] = dkp
                else: dv[...] += dvp; dk[...] += dkp
                if mode == "tn":
                    dq[i] += tn(ds, kt)
                else:
                    dq[i] += tn(kt, ds)
            block(j, True, True)
            def qstep(i, _):
                block(i, False, False); return 0
            lax.fori_loop(j + 1, nb, qstep, 0)
            out[ks, W + p * 128:W + (p + 1) * 128] = dk[...].astype(bf16)
            out[ks, 2 * W + p * 128:2 * W + (p + 1) * 128] = dv[...].astype(bf16)
            return 0
        lax.fori_loop(0, nb, kstep, 0)
        def fin(i, _, p=p):
            qs = pl.ds(pl.multiple_of(i * B, B), B)
            if mode == "tn":
                d = dq[i]
                r = jnp.where(half, d[:B], d[B:])
            else:
                d = dq[i]
                r = jnp.concatenate([d[:64, :B], d[64:, B:]], axis=0).T
            out[qs, p * 128:(p + 1) * 128] = (r * 0.125).astype(bf16)
            return 0
        lax.fori_loop(0, nb, fin, 0)

def attn_bwd(lengths, qkv, do, lse, dl, B=256, mode="tn"):
    rows, w3 = qkv.shape; W = w3 // 3; pairs = W // 128; nb = rows // B
    dqs = (nb, 2 * B, 128) if mode == "tn" else (nb, 128, 2 * B)
    return pl.pallas_call(functools.partial(bwd_kernel, B=B, pairs=pairs, mode=mode), name="attn_bwd",
        out_shape=jax.ShapeDtypeStruct((rows, w3), bf16),
        in_specs=[pl.BlockSpec(memory_space=pltpu.SMEM)] + [pl.BlockSpec(memory_space=pltpu.VMEM)] * 4,
        out_specs=pl.BlockSpec(memory_space=pltpu.VMEM),
        scratch_shapes=[pltpu.VMEM((rows, 128), bf16), pltpu.VMEM((rows, 128), bf16), pltpu.VMEM((nb, 2 * B, 256), bf16),
                        pltpu.VMEM((nb, 2 * B, 128), bf16), pltpu.VMEM(dqs, f32), pltpu.VMEM((B, 128), f32), pltpu.VMEM((B, 128), f32)],
        compiler_params=pltpu.CompilerParams(vmem_limit_bytes=56 << 20))(lengths, qkv, do, lse, dl)

def stats(v):
    n = v.shape[-1]
    m = jnp.sum(v, axis=-1, keepdims=True) * (1.0 / n)
    c = v - m
    s = jnp.sum(c * c, axis=-1, keepdims=True) * (1.0 / n)
    r = lax.rsqrt(s + EPS)
    return c * r, r
def ln_back(w, vh, r, g):
    n = vh.shape[-1]
    wg = w * g
    a = jnp.sum(wg, axis=-1, keepdims=True) * (1.0 / n)
    b = jnp.sum(wg * vh, axis=-1, keepdims=True) * (1.0 / n)
    return r * (wg - a - vh * b)
def gelu_parts(h):
    e = jnp.exp(h * h * -0.5)
    d = 1.0 + jnp.abs(h) * 0.23164189
    t = pl.reciprocal(d, approx=True)
    t = t * (2.0 - d * t)
    y = t * (0.127414796 + t * (-0.142248368 + t * (0.710706870 + t * (-0.726576013 + t * 0.530702714))))
    q = y * e
    return jnp.where(h >= 0, 1.0 - q, q), e * 0.3989422804014327
def colsum(v): return jnp.sum(v, axis=0, keepdims=True)

def ffn_kernel(o_ref, x_ref, g_ref, gall_ref, wo, fc1, fc2, vec, mg, mb, sel,
               out_ref, dy_ref, do_ref, delta_ref, gwo, gfc1, gfc2, gvec, gmg, gmb,
               u_s, d_s, m_s, dh_s, c_s, b_s, db_s, e_s, *, T, NT, NC):
    step = pl.program_id(0)
    K = fc1.shape[1]
    ff = NC * K
    @pl.when(step < NT)
    def _():
        rs = pl.ds(pl.multiple_of(step * T, T), T)
        @pl.when(step == 0)
        def _():
            gvec[...] = jnp.zeros_like(gvec); gmg[...] = jnp.zeros_like(gmg); gmb[...] = jnp.zeros_like(gmb)
        sg, sb, fg, fb = [vec[k:k + 1, :] for k in range(4)]
        o = o_ref[...].astype(f32)
        oh, orr = stats(o)
        b = (oh * sg + sb).astype(bf16)
        b_s[rs, :] = b
        y = x_ref[...].astype(f32) + nn(b, wo[...])
        yh, yr = stats(y)
        cc = (yh * fg + fb).astype(bf16)
        c_s[rs, :] = cc
        g = g_ref[...]
        def pass_a(c, st):
            s1, s2 = st
            h = nt(c_s[rs, :], fc1[c])
            phi, den = gelu_parts(h)
            u = h * phi
            u_s[c] = u
            d_s[c] = phi + h * den
            return s1 + jnp.sum(u, axis=1, keepdims=True), s2 + jnp.sum(u * u, axis=1, keepdims=True)
        z1 = jnp.zeros((T, 1), f32)
        s1, s2 = lax.fori_loop(0, NC, pass_a, (z1, z1))
        mu = s1 * (1.0 / ff)
        R = lax.rsqrt(s2 * (1.0 / ff) - mu * mu + EPS)
        def pass_b(c, st):
            acc, se, seu = st
            uh = (u_s[c] - mu) * R
            u_s[c] = uh
            gain = mg[c]
            m = (uh * gain + mb[c]).astype(bf16)
            m_s[c, rs, :] = m
            acc = acc + nn(m, fc2[c])
            dm = nt(g_ref[...], fc2[c])
            t = dm * uh
            gmg[c] += colsum(t)
            gmb[c] += colsum(dm)
            e = dm * gain
            e_s[c] = e
            return acc, se + jnp.sum(e, axis=1, keepdims=True), seu + jnp.sum(e * uh, axis=1, keepdims=True)
        acc, se, seu = lax.fori_loop(0, NC, pass_b, (y, z1, z1))
        out_ref[...] = acc.astype(bf16)
        se = se * (1.0 / ff); seu = seu * (1.0 / ff)
        def pass_c(c, acc):
            dh = ((e_s[c] - se - u_s[c] * seu) * R * d_s[c]).astype(bf16)
            dh_s[c, rs, :] = dh
            return acc + nn(dh, fc1[c])
        dc = lax.fori_loop(0, NC, pass_c, jnp.zeros((T, fc1.shape[2]), f32))
        gvec[2:3] += colsum(dc * yh)
        gvec[3:4] += colsum(dc)
        dy = g.astype(f32) + ln_back(dc, yh, yr, fg)
        dy_ref[...] = dy
        db = dy.astype(bf16)
        db_s[rs, :] = db
        dbn = nt(db, wo[...])
        gvec[0:1] += colsum(dbn * oh)
        gvec[1:2] += colsum(dbn)
        do = ln_back(dbn, oh, orr, sg).astype(bf16)
        do_ref[...] = do
        pr = do.astype(f32) * o
        hi = pr.astype(bf16)
        lo = (pr - hi.astype(f32)).astype(bf16)
        delta_ref[...] = nt(sel[...], hi) + nt(sel[...], lo)
    @pl.when(step >= NT)
    def _():
        c = step - NT
        gfc2[0] = tn(m_s[c], gall_ref[...]).astype(bf16)
        gfc1[0] = tn(dh_s[c], c_s[...]).astype(bf16)
        @pl.when(step == NT)
        def _():
            gwo[...] = tn(b_s[...], db_s[...]).astype(bf16)

def ffn(o, x, g, wo, fc1, fc2, vec, mg, mb, T=256, K=512):
    rows, D = x.shape; ff = fc1.shape[0]; NC = ff // K; NT = rows // T
    head = jnp.arange(D)[None] // 64
    sel = (jnp.arange(16)[:, None] == head // (D // 128) * 8 + head % (D // 128)).astype(bf16)
    fc1 = fc1.reshape(NC, K, D); fc2 = fc2.reshape(NC, K, D)
    mg = mg.reshape(NC, 1, K); mb = mb.reshape(NC, 1, K)
    row = lambda s: (jnp.minimum(s, NT - 1), 0)
    cst2 = lambda s: (0, 0)
    cst3 = lambda s: (0, 0, 0)
    one = dict(pipeline_mode=pl.Buffered(1))
    chunk = lambda s: (jnp.maximum(s - NT, 0), 0, 0)
    return pl.pallas_call(functools.partial(ffn_kernel, T=T, NT=NT, NC=NC), name="ffn",
        grid=(NT + NC,),
        in_specs=[pl.BlockSpec((T, D), row), pl.BlockSpec((T, D), row), pl.BlockSpec((T, D), row),
                  pl.BlockSpec((rows, D), cst2, **one), pl.BlockSpec((D, D), cst2, **one),
                  pl.BlockSpec((NC, K, D), cst3, **one), pl.BlockSpec((NC, K, D), cst3, **one),
                  pl.BlockSpec((8, D), cst2, **one), pl.BlockSpec((NC, 1, K), cst3, **one), pl.BlockSpec((NC, 1, K), cst3, **one),
                  pl.BlockSpec((16, D), cst2, **one)],
        out_specs=[pl.BlockSpec((T, D), row), pl.BlockSpec((T, D), row), pl.BlockSpec((T, D), row),
                   pl.BlockSpec((16, T), lambda s: (0, jnp.minimum(s, NT - 1))),
                   pl.BlockSpec((D, D), cst2, **one), pl.BlockSpec((1, K, D), chunk), pl.BlockSpec((1, K, D), chunk),
                   pl.BlockSpec((8, D), cst2, **one), pl.BlockSpec((NC, 1, K), cst3, **one), pl.BlockSpec((NC, 1, K), cst3, **one)],
        out_shape=[jax.ShapeDtypeStruct((rows, D), bf16), jax.ShapeDtypeStruct((rows, D), f32), jax.ShapeDtypeStruct((rows, D), bf16),
                   jax.ShapeDtypeStruct((16, rows), f32), jax.ShapeDtypeStruct((D, D), bf16),
                   jax.ShapeDtypeStruct((NC, K, D), bf16), jax.ShapeDtypeStruct((NC, K, D), bf16),
                   jax.ShapeDtypeStruct((8, D), f32), jax.ShapeDtypeStruct((NC, 1, K), f32), jax.ShapeDtypeStruct((NC, 1, K), f32)],
        scratch_shapes=[pltpu.VMEM((NC, T, K), f32), pltpu.VMEM((NC, T, K), f32), pltpu.VMEM((NC, rows, K), bf16), pltpu.VMEM((NC, rows, K), bf16),
                        pltpu.VMEM((rows, D), bf16), pltpu.VMEM((rows, D), bf16), pltpu.VMEM((rows, D), bf16), pltpu.VMEM((NC, T, K), f32)],
        compiler_params=pltpu.CompilerParams(vmem_limit_bytes=62 << 20, dimension_semantics=("arbitrary",)))(
            o, x, g, g, wo, fc1, fc2, vec, mg, mb, sel)

def norm(v):
    return stats(v)


def local(tokens, cotangent, lengths, qkv_weight, out_weight, pre_gain, pre_shift, sub_gain, sub_shift,
          ffn_gain, ffn_shift, fc1_weight, mid_gain, mid_shift, fc2_weight):
    rows, D = tokens.shape
    W = D // 2
    tp = lax.axis_index("tp")
    both = ("dp", "tp")
    gather = lambda a: lax.all_gather(a, both, axis=0, tiled=True)
    small = gather(jnp.stack([pre_gain, pre_shift, sub_gain, sub_shift, ffn_gain, ffn_shift], axis=1)).astype(f32).T
    mid = gather(jnp.stack([mid_gain, mid_shift], axis=1)).astype(f32).T
    wq = gather(qkv_weight)
    wo, fc1, fc2 = gather(out_weight), gather(fc1_weight), gather(fc2_weight)
    wown = lax.dynamic_index_in_dim(wq.reshape(D, 3, 2, W), tp, 2, keepdims=False).reshape(D, 3 * W)
    x = tokens.astype(f32)
    xh, xr = norm(x)
    a = (xh * small[0] + small[1]).astype(bf16)
    afull = lax.all_gather(a, "tp", axis=0, tiled=True)
    qkv = nn(afull, wown).astype(bf16)
    o_own, lse = attn_fwd(lengths, qkv, B=512)
    o = lax.all_to_all(o_own, "tp", 0, 1, tiled=True)
    vec = jnp.concatenate([small[2:6], jnp.zeros((4, D), f32)], axis=0)
    block_out, dy, do, delta, gwo, gfc1, gfc2, gvec, gmg, gmb = ffn(o, tokens, cotangent, wo, fc1, fc2, vec, mid[0], mid[1])
    do_own = lax.all_to_all(do, "tp", 1, 0, tiled=True)
    dl_own = lax.all_to_all(delta, "tp", 0, 1, tiled=True)
    dqkv = attn_bwd(lengths, qkv, do_own, lse, dl_own, B=512)
    gq = tn(afull, dqkv)
    da = lax.psum_scatter(nt(dqkv, wown), "tp", scatter_dimension=0, tiled=True)
    grad_tokens = (dy + ln_back(da, xh, xr, small[0])).astype(bf16)
    scatter = lambda v: lax.psum_scatter(v, both, scatter_dimension=0, tiled=True)
    gq = lax.psum_scatter(gq, "dp", scatter_dimension=0, tiled=True)
    n = gq.shape[0] // 2
    gq = lax.all_to_all(gq.reshape(2, n, 3, 1, W), "tp", 0, 3, tiled=True).reshape(n, 3 * D)
    small_grads = scatter(jnp.concatenate([jnp.stack([colsum(da * xh)[0], colsum(da)[0]]), gvec[:4]], axis=0).T).T
    mid_grads = scatter(jnp.stack([gmg.reshape(-1), gmb.reshape(-1)], axis=1)).T
    gwo = scatter(gwo.astype(f32))
    gfc1 = scatter(gfc1.reshape(-1, D).astype(f32))
    gfc2 = scatter(gfc2.reshape(-1, D).astype(f32))
    return (block_out, grad_tokens, gq, gwo, small_grads[0], small_grads[1], small_grads[2], small_grads[3],
            small_grads[4], small_grads[5], gfc1, mid_grads[0], mid_grads[1], gfc2)


def solution(mesh):
    two, one = P(("dp", "tp"), None), P(("dp", "tp"))
    return jax.shard_map(
        local,
        mesh=mesh,
        in_specs=(two, two, P("dp", None), two, two, one, one, one, one, one, one, two, one, one, two),
        out_specs=(two, two, two, two, one, one, one, one, one, one, two, one, one, two),
        check_vma=False,
    )
```

time: 1470 us -> 1030 us (0.70)
  matrix products: 376 us -> 25.6 us
  local copies, waits for them, and re-layouts: 268 us -> 21.4 us
  waiting for transfers between devices: 393 us -> 614 us
  Pallas kernels: 0 us -> 179 us
  other arithmetic: 199 us -> 27.2 us
  blocking collectives: 208 us -> 136 us
    dot_general x96 -> x3, matrix products: 376 us -> 25.6 us  [the longest x1 8.86 us: nn(): lax.dot_general(a, b, (((1,), (0,)), ((), ())), preferred_element_type=f32)]
    pallas_call x0 -> x3, Pallas kernels: none -> 179 us  [the longest x1 86.6 us: ffn(): pl.pallas_call(functools.partial(ffn_kernel, T=T, NT=NT, NC=NC), name='ff...]
    unnamed x4 -> x1, blocking collectives: 201 us -> 40.7 us
    reduce_scatter x8 -> x5, waiting for transfers between devices: 358 us -> 488 us  [the longest x3 341 us: local(): lax.psum_scatter(v, both, scatter_dimension=0, tiled=True)]
    all_gather x8 -> x5, waiting for transfers between devices: 31.4 us -> 119 us  [the longest x4 119 us: local(): gather = lambda a: lax.all_gather(a, both, axis=0, tiled=True)]
    all_gather x0 -> x2, blocking collectives: none -> 80.5 us  [local(): gather = lambda a: lax.all_gather(a, both, axis=0, tiled=True)]
    dynamic_slice x144 -> x1, local copies, waits for them, and re-layouts: 78.5 us -> 1.34 us  [local(): lax.dynamic_index_in_dim(wq.reshape(D, 3, 2, W), tp, 2, keepdims=False)]
    dynamic_update_slice x24 -> x0, local copies, waits for them, and re-layouts: 71.4 us -> none  [the longest x12 36.3 us: forward_step(): mixed_all = lax.dynamic_update_slice(mixed_all, mixed, (first_row, column))]
  transfers between devices with their start and end apart: 16 -> 12, of which waited for: 7 -> 9; matrix products, arithmetic and copies ran while one was open for 23% -> 7% of each run, Pallas kernels for 0% -> 9%
where the time goes in v1:
time: 1030 us; the launch traced here: 1020 us
  waiting for transfers between devices  614 us (60%)
  Pallas kernels  179 us (17%)
  blocking collectives  136 us (13%)
  other arithmetic  27.2 us (3%)
  matrix products  25.6 us (2%)
  local copies, waits for them, and re-layouts  21.4 us (2%)
  between operations  14.4 us (1%)
    reduce_scatter x3, waiting for transfers between devices, local(): lax.psum_scatter(v, both, scatter_dimension=0, tiled=True)  341 us
    reduce_scatter x1, waiting for transfers between devices, local(): gq = lax.psum_scatter(gq, 'dp', scatter_dimension=0, tiled=True)  137 us
    all_gather x4, waiting for transfers between devices, local(): gather = lambda a: lax.all_gather(a, both, axis=0, tiled=True)  119 us
    pallas_call x1, Pallas kernels, ffn(): pl.pallas_call(functools.partial(ffn_kernel, T=T, NT=NT, NC=NC), name='ff...  86.6 us
    all_gather x2, blocking collectives, local(): gather = lambda a: lax.all_gather(a, both, axis=0, tiled=True)  80.5 us
    pallas_call x1, Pallas kernels, attn_bwd(): pl.pallas_call(functools.partial(bwd_kernel, B=B, pairs=pairs, mode=mode)...  56.3 us
    unnamed x1, blocking collectives  40.7 us
    pallas_call x1, Pallas kernels, attn_fwd(): pl.pallas_call(functools.partial(fwd_t, B=B, pairs=pairs, variant=variant...  36.2 us
  transfers between devices with their start and end apart: 12, of which 9 were waited for; matrix products, arithmetic and copies ran while one was open for 7% of the time, Pallas kernels for 9%

profile of v1, /device:TPU:0, one launch (start us, length us, event | category | flops | bytes accessed | tf_op | source)
XLA Modules:
  0.0 1021.7 jit_solution(8873936600670653841)
XLA Ops:
  8.7 43.5 %all-gather = bf16[32,24,6]{1,2,0:T(8,128)(2,1)S(1)} all-gather(bf16[1,24,6]{1,2,0:T(8,128)(2,1)S(1)} %bitcast.101), channel_id=1, replica_groups=mesh['dp'=16,'tp'=2] {'dp','tp'}, dimensions={0}, use_global_device_ids=true | all-gather | bytes 9504 | tf_op jit(solution)/shard_map/all_gather | solution.py:341
  58.7 37.0 %all-gather.1 = bf16[32,96,2]{1,2,0:T(2,128)(2,1)S(1)} all-gather(bf16[1,96,2]{1,2,0:T(2,128)(2,1)S(1)} %maximum_bitcast_fusion.1), channel_id=1, replica_groups=mesh['dp'=16,'tp'=2] {'dp','tp'}, dimensions={0}, use_global_device_ids=true | all-gather | bytes 12672 | tf_op jit(solution)/shard_map/all_gather | solution.py:341
  97.7 4.5 copy.52
  103.6 8.9 convolution_convert_fusion.qkv
  112.4 36.2 %attn_fwd.1 = (bf16[2048,384]{1,0:T(8,128)(2,1)}, f32[8,2048]{1,0:T(8,128)}) custom-call(s32[1,8]{1,0:T(1,128)} %len_ref.3, bf16[2048,1152]{1,0:T(8,128)(2,1)} %convolution_convert_fusion.qkv), custom_call_target="tpu_custom_call" | custom-call | tf_op jit(solution)/shard_map/attn_fwd/pallas_call | solution.py:113
  148.6 6.3 all_to_all.72
  156.2 54.2 %all-gather.14.cloned.1.call-done = bf16[3072,768]{1,0:T(8,128)(2,1)} async-done(((bf16[96,768]{1,0:T(8,128)(2,1)}), bf16[3072,768]{1,0:T(8,128)(2,1)}) %all-gather.14.cloned.1.call-update) | async-done | bytes 4718608 | tf_op jit(solution)/shard_map/all_gather | solution.py:341
  210.5 65.2 %all-gather.16.cloned.1.call-done = bf16[3072,768]{1,0:T(8,128)(2,1)} async-done(((bf16[96,768]{1,0:T(8,128)(2,1)}), bf16[3072,768]{1,0:T(8,128)(2,1)}) %all-gather.16.cloned.1.call-update) | async-done | bytes 4718608 | tf_op jit(solution)/shard_map/all_gather | solution.py:341
  275.7 86.6 %ffn.1 = (bf16[1024,768]{1,0:T(8,128)(2,1)}, f32[1024,768]{1,0:T(8,128)}, bf16[1024,768]{1,0:T(8,128)(2,1)}, f32[16,1024]{1,0:T(8,128)}, bf16[768,768]{1,0:T(8,1...) custom-call(bf16[1024,768]{1,0:T(8,128)(2,1)} %bitcast.84, ...), custom_call_target="tpu_custom_call" | custom-call | tf_op jit(solution)/shard_map/ffn/pallas_call | solution.py:311
  365.0 3.8 all-to-all-start.1
  371.3 4.7 all_to_all.73
  376.0 56.3 %attn_bwd.1 = bf16[2048,1152]{1,0:T(8,128)(2,1)} custom-call(s32[1,8]{1,0:T(1,128)} %len_ref.3, bf16[2048,1152]{1,0:T(8,128)(2,1)} %convolution_convert_fusion.qkv, bf16[2048,384]{1,0:T(8,128)(2,1)} %bitcast.83, f32[8,2048]{1,0:T(8,128)} %get-tuple-element.30.lse_ref, f32[8,2048]{1,0:T(8,128)} %bitcast.92), custom_call_target="tpu_custom_call" | custom-call | tf_op jit(solution)/shard_map/attn_bwd/pallas_call | solution.py:188
  432.3 8.4 fusion.31
  442.2 8.4 fusion.30
  453.5 6.7 bitcast_convert_fusion.1
  460.3 6.7 bitcast_convert_fusion
  472.0 137.0 %reduce-scatter.12.cloned.1.call-done = f32[48,1152]{1,0:T(8,128)} async-done(((f32[768,1152]{1,0:T(8,128)}), f32[48,1152]{1,0:T(8,128)}) %reduce-scatter.12.cloned.1.call-update) | async-done | bytes 221200 | tf_op jit(solution)/shard_map/reduce_scatter | solution.py:363
  610.0 3.9 all_to_all.74
  614.9 10.2 reduce-scatter.10.cloned.1.call-done
  628.2 40.7 %all-reduce.1 = f32[768,6]{0,1:T(8,128)S(1)} all-reduce(f32[768,6]{0,1:T(8,128)S(1)} %maximum_bitcast_fusion), channel_id=5, replica_groups=mesh['dp'=16,'tp'=2] {'dp','tp'}, use_global_device_ids=true, to_apply=%region_9.10.clone | all-reduce | flops 4608 | bytes 36864
  669.5 4.4 fusion.12
  673.9 58.1 %reduce-scatter.14.cloned.1.call-done = f32[24,768]{1,0:T(8,128)} async-done(((f32[768,768]{1,0:T(8,128)}), f32[24,768]{1,0:T(8,128)}) %reduce-scatter.14.cloned.1.call-update) | async-done | bytes 73744 | tf_op jit(solution)/shard_map/reduce_scatter | solution.py:362
  732.0 140.8 %reduce-scatter.16.cloned.1.call-done = f32[96,768]{1,0:T(8,128)} async-done(((f32[3072,768]{1,0:T(8,128)}), f32[96,768]{1,0:T(8,128)}) %reduce-scatter.16.cloned.1.call-update) | async-done | bytes 294928 | tf_op jit(solution)/shard_map/reduce_scatter | solution.py:362
  872.8 142.1 %reduce-scatter.18.cloned.1.call-done = f32[96,768]{1,0:T(8,128)} async-done(((f32[3072,768]{1,0:T(8,128)}), f32[96,768]{1,0:T(8,128)}) %reduce-scatter.18.cloned.1.call-update) | async-done | bytes 294928 | tf_op jit(solution)/shard_map/reduce_scatter | solution.py:362
  (89 shorter events, 32.7 us)
Async XLA Ops:
  7.2 47.1 %copy-start = (bf16[1024,768]{1,0:T(8,128)(2,1)S(1)}, bf16[1024,768]{1,0:T(8,128)(2,1)}, u32[]{:S(2)}) copy-start(bf16[1024,768]{1,0:T(8,128)(2,1)} %x_ref.1) | copy-start | bytes 4718596
  7.2 90.5 %all-gather.10.cloned.1.call-start = ((), (), s32[]{:S(2)}) async-start(), calls=%async_computation.11 | async-start | bytes 3649536 | tf_op jit(solution)/shard_map/all_gather | solution.py:341
  7.9 95.6 %all-gather.8.cloned.1.call-start = ((), (), s32[]{:S(2)}) async-start(), calls=%async_computation.10 | async-start | bytes 4718592 | tf_op jit(solution)/shard_map/all_gather | solution.py:350
  54.3 4.4 copy-start.10
  54.3 4.4 copy-start.11
  56.8 99.5 %all-gather.12.cloned.1.call-start = ((), (), s32[]{:S(2)}) async-start(), calls=%async_computation.12 | async-start | bytes 1216512 | tf_op jit(solution)/shard_map/all_gather | solution.py:341
  57.5 153.0 %all-gather.14.cloned.1.call-start = ((), (), s32[]{:S(2)}) async-start(), calls=%async_computation.13 | async-start | bytes 4866048 | tf_op jit(solution)/shard_map/all_gather | solution.py:341
  58.1 217.6 %all-gather.16.cloned.1.call-start = ((), (), s32[]{:S(2)}) async-start(), calls=%async_computation.14 | async-start | bytes 4866048 | tf_op jit(solution)/shard_map/all_gather | solution.py:341
  362.3 6.6 copy-start.6
  362.3 6.6 copy-start.7
  365.0 6.3 copy-start.5
  365.0 6.3 all-to-all-start.1
  368.8 101.8 %reduce-scatter.20.cloned.1.call-start = ((), (), s32[]{:S(2)}) async-start(), calls=%async_computation.20 | async-start | bytes 1622016
  370.6 238.4 %reduce-scatter.12.cloned.1.call-start = ((), (), s32[]{:S(2)}) async-start(), calls=%async_computation.16 | async-start | bytes 3760128 | tf_op jit(solution)/shard_map/reduce_scatter | solution.py:363
  371.3 4.7 copy-start.2
  376.0 56.3 %copy-start.9 = (bf16[2048,768]{1,0:T(8,128)(2,1)S(1)}, bf16[2048,768]{1,0:T(8,128)(2,1)}, u32[]{:S(2)}) copy-start(bf16[2048,768]{1,0:T(8,128)(2,1)} %all-gather.8.cloned.1.call-done) | copy-start | bytes 9437188
  440.7 1.5 copy-start.3
  440.7 184.4 %reduce-scatter.10.cloned.1.call-start = ((), (), s32[]{:S(2)}) async-start(), calls=%async_computation.15 | async-start | bytes 9437184 | tf_op jit(solution)/shard_map/reduce_scatter | solution.py:360
  450.5 1.3 copy-start.4
  450.6 281.5 %reduce-scatter.14.cloned.1.call-start = ((), (), s32[]{:S(2)}) async-start(), calls=%async_computation.17 | async-start | bytes 2433024 | tf_op jit(solution)/shard_map/reduce_scatter | solution.py:362
  453.4 419.4 %reduce-scatter.16.cloned.1.call-start = ((), (), s32[]{:S(2)}) async-start(), calls=%async_computation.18 | async-start | bytes 9732096 | tf_op jit(solution)/shard_map/reduce_scatter | solution.py:362
  460.2 554.7 %reduce-scatter.18.cloned.1.call-start = ((), (), s32[]{:S(2)}) async-start(), calls=%async_computation.19 | async-start | bytes 9732096 | tf_op jit(solution)/shard_map/reduce_scatter | solution.py:362
  467.0 0.7 copy-start.8
  467.0 158.1 %copy-start.1 = (bf16[1024,768]{1,0:T(8,128)(2,1)S(1)}, bf16[1024,768]{1,0:T(8,128)(2,1)}, u32[]{:S(2)}) copy-start(bf16[1024,768]{1,0:T(8,128)(2,1)} %x_ref.1) | copy-start | bytes 4718596
Sparse Core Ops, SparseCore 0:
  10.9 62.9 all-gather.9
  76.0 10.9 all-gather.7
  89.9 55.1 all-gather.11
  147.9 62.5 all-gather.13
  213.2 62.4 all-gather.15
  374.6 95.9 reduce-scatter.19
  475.7 133.2 reduce-scatter.11
  611.3 13.7 reduce-scatter.9
  631.8 100.1 reduce-scatter.13
  738.3 134.4 reduce-scatter.15
  880.3 134.6 reduce-scatter.17

commit v2 on v1

--- a/solution.py
+++ b/solution.py
@@ -2,6 +2,7 @@
 
 import jax
 import jax.numpy as jnp
+import numpy as np
 from jax import lax
 from jax.experimental import pallas as pl
 from jax.experimental.pallas import tpu as pltpu
@@ -216,8 +217,8 @@
     return jnp.where(h >= 0, 1.0 - q, q), e * 0.3989422804014327
 def colsum(v): return jnp.sum(v, axis=0, keepdims=True)
 
-def ffn_kernel(o_ref, x_ref, g_ref, gall_ref, wo, fc1, fc2, vec, mg, mb, sel,
-               out_ref, dy_ref, do_ref, delta_ref, gwo, gfc1, gfc2, gvec, gmg, gmb,
+def ffn_kernel(o_ref, x_ref, g_ref, gall_ref, wo, fc1, fc2, vec, mid, sel,
+               out_ref, dy_ref, do_ref, delta_ref, gwo, gfc1, gfc2, gvec, gmid,
                u_s, d_s, m_s, dh_s, c_s, b_s, db_s, e_s, *, T, NT, NC):
     step = pl.program_id(0)
     K = fc1.shape[1]
@@ -227,8 +228,8 @@
         rs = pl.ds(pl.multiple_of(step * T, T), T)
         @pl.when(step == 0)
         def _():
-            gvec[...] = jnp.zeros_like(gvec); gmg[...] = jnp.zeros_like(gmg); gmb[...] = jnp.zeros_like(gmb)
-        sg, sb, fg, fb = [vec[k:k + 1, :] for k in range(4)]
+            gvec[...] = jnp.zeros_like(gvec); gmid[...] = jnp.zeros_like(gmid)
+        sg, sb, fg, fb = [vec[k:k + 1, :] for k in range(2, 6)]
         o = o_ref[...].astype(f32)
         oh, orr = stats(o)
         b = (oh * sg + sb).astype(bf16)
@@ -254,14 +255,15 @@
             acc, se, seu = st
             uh = (u_s[c] - mu) * R
             u_s[c] = uh
-            gain = mg[c]
-            m = (uh * gain + mb[c]).astype(bf16)
+            lanes = pl.ds(pl.multiple_of(c * K, K), K)
+            gain = mid[0:1, lanes]
+            m = (uh * gain + mid[1:2, lanes]).astype(bf16)
             m_s[c, rs, :] = m
             acc = acc + nn(m, fc2[c])
             dm = nt(g_ref[...], fc2[c])
             t = dm * uh
-            gmg[c] += colsum(t)
-            gmb[c] += colsum(dm)
+            gmid[6:7, lanes] += colsum(t)
+            gmid[7:8, lanes] += colsum(dm)
             e = dm * gain
             e_s[c] = e
             return acc, se + jnp.sum(e, axis=1, keepdims=True), seu + jnp.sum(e * uh, axis=1, keepdims=True)
@@ -273,15 +275,15 @@
             dh_s[c, rs, :] = dh
             return acc + nn(dh, fc1[c])
         dc = lax.fori_loop(0, NC, pass_c, jnp.zeros((T, fc1.shape[2]), f32))
-        gvec[2:3] += colsum(dc * yh)
-        gvec[3:4] += colsum(dc)
+        gvec[4:5, :] += colsum(dc * yh)
+        gvec[5:6, :] += colsum(dc)
         dy = g.astype(f32) + ln_back(dc, yh, yr, fg)
-        dy_ref[...] = dy
         db = dy.astype(bf16)
+        dy_ref[...] = db
         db_s[rs, :] = db
         dbn = nt(db, wo[...])
-        gvec[0:1] += colsum(dbn * oh)
-        gvec[1:2] += colsum(dbn)
+        gvec[2:3, :] += colsum(dbn * oh)
+        gvec[3:4, :] += colsum(dbn)
         do = ln_back(dbn, oh, orr, sg).astype(bf16)
         do_ref[...] = do
         pr = do.astype(f32) * o
@@ -297,12 +299,11 @@
         def _():
             gwo[...] = tn(b_s[...], db_s[...]).astype(bf16)
 
-def ffn(o, x, g, wo, fc1, fc2, vec, mg, mb, T=256, K=512):
+def ffn(o, x, g, wo, fc1, fc2, vec, mid, T=256, K=512):
     rows, D = x.shape; ff = fc1.shape[0]; NC = ff // K; NT = rows // T
-    head = jnp.arange(D)[None] // 64
-    sel = (jnp.arange(16)[:, None] == head // (D // 128) * 8 + head % (D // 128)).astype(bf16)
+    head = np.arange(D)[None] // 64
+    sel = jnp.asarray((np.arange(16)[:, None] == head // (D // 128) * 8 + head % (D // 128)).astype(np.float32), bf16)
     fc1 = fc1.reshape(NC, K, D); fc2 = fc2.reshape(NC, K, D)
-    mg = mg.reshape(NC, 1, K); mb = mb.reshape(NC, 1, K)
     row = lambda s: (jnp.minimum(s, NT - 1), 0)
     cst2 = lambda s: (0, 0)
     cst3 = lambda s: (0, 0, 0)
@@ -313,26 +314,551 @@
         in_specs=[pl.BlockSpec((T, D), row), pl.BlockSpec((T, D), row), pl.BlockSpec((T, D), row),
                   pl.BlockSpec((rows, D), cst2, **one), pl.BlockSpec((D, D), cst2, **one),
                   pl.BlockSpec((NC, K, D), cst3, **one), pl.BlockSpec((NC, K, D), cst3, **one),
-                  pl.BlockSpec((8, D), cst2, **one), pl.BlockSpec((NC, 1, K), cst3, **one), pl.BlockSpec((NC, 1, K), cst3, **one),
+                  pl.BlockSpec((8, D), cst2, **one), pl.BlockSpec((8, ff), cst2, **one),
                   pl.BlockSpec((16, D), cst2, **one)],
         out_specs=[pl.BlockSpec((T, D), row), pl.BlockSpec((T, D), row), pl.BlockSpec((T, D), row),
                    pl.BlockSpec((16, T), lambda s: (0, jnp.minimum(s, NT - 1))),
                    pl.BlockSpec((D, D), cst2, **one), pl.BlockSpec((1, K, D), chunk), pl.BlockSpec((1, K, D), chunk),
-                   pl.BlockSpec((8, D), cst2, **one), pl.BlockSpec((NC, 1, K), cst3, **one), pl.BlockSpec((NC, 1, K), cst3, **one)],
-        out_shape=[jax.ShapeDtypeStruct((rows, D), bf16), jax.ShapeDtypeStruct((rows, D), f32), jax.ShapeDtypeStruct((rows, D), bf16),
+                   pl.BlockSpec((8, D), cst2, **one), pl.BlockSpec((8, ff), cst2, **one)],
+        out_shape=[jax.ShapeDtypeStruct((rows, D), bf16), jax.ShapeDtypeStruct((rows, D), bf16), jax.ShapeDtypeStruct((rows, D), bf16),
                    jax.ShapeDtypeStruct((16, rows), f32), jax.ShapeDtypeStruct((D, D), bf16),
                    jax.ShapeDtypeStruct((NC, K, D), bf16), jax.ShapeDtypeStruct((NC, K, D), bf16),
-                   jax.ShapeDtypeStruct((8, D), f32), jax.ShapeDtypeStruct((NC, 1, K), f32), jax.ShapeDtypeStruct((NC, 1, K), f32)],
+                   jax.ShapeDtypeStruct((8, D), f32), jax.ShapeDtypeStruct((8, ff), f32)],
         scratch_shapes=[pltpu.VMEM((NC, T, K), f32), pltpu.VMEM((NC, T, K), f32), pltpu.VMEM((NC, rows, K), bf16), pltpu.VMEM((NC, rows, K), bf16),
                         pltpu.VMEM((rows, D), bf16), pltpu.VMEM((rows, D), bf16), pltpu.VMEM((rows, D), bf16), pltpu.VMEM((NC, T, K), f32)],
         compiler_params=pltpu.CompilerParams(vmem_limit_bytes=62 << 20, dimension_semantics=("arbitrary",)))(
-            o, x, g, g, wo, fc1, fc2, vec, mg, mb, sel)
+            o, x, g, g, wo, fc1, fc2, vec, mid, sel)
+
+MESH = pl.DeviceIdType.MESH
+
+def place():
+    dp, tp = lax.axis_index("dp"), lax.axis_index("tp")
+    q, z = dp % 4, dp // 4
+    dx = 1 - 2 * (dp % 2)
+    dy = 2 - 4 * ((dp // 2) % 2)
+    a, b = (1 - tp) * dx + tp * dy, tp * dx + (1 - tp) * dy
+    return dict(dp=dp, tp=tp, z=z, q=q, qa=q + a, qb=q + b, qab=q + a + b,
+                a=(dp + a, tp), b=(dp + b, tp), peer=(dp, 1 - tp),
+                zs=[((dp + 4 * k) % 16, tp) for k in (1, 2, 3)], zi=[(z + k) % 4 for k in (1, 2, 3)])
+
+def enter(w):
+    bar = pltpu.get_barrier_semaphore()
+    for d in [w["a"], w["b"], w["peer"]] + w["zs"]:
+        pl.semaphore_signal(bar, inc=1, device_id=d, device_id_type=MESH)
+    pl.semaphore_wait(bar, 6)
+
+class Sender:
+    def __init__(self, ss, rs):
+        self.ss, self.rs, self.n, self.all = ss, rs, 0, []
+    def __call__(self, src, dst, dev):
+        c = pltpu.make_async_remote_copy(src_ref=src, dst_ref=dst, send_sem=self.ss.at[self.n], recv_sem=self.rs.at[self.n],
+                                         device_id=dev, device_id_type=MESH)
+        self.n += 1
+        self.all.append(c)
+        c.start()
+        return c
+
+class Gather:
+    def __init__(self, send, w, src, slot, view, peer):
+        self.send, self.w, self.src, self.slot, self.view, self.peer = send, w, src, slot, view, peer
+    def plan(self):
+        pass
+    def start(self):
+        w = self.w
+        s = self.slot(w["z"], w["q"], w["tp"])
+        self.cz = [self.send(self.src, s, d) for d in w["zs"]]
+    def _fan(self, q, devs):
+        v = self.view(q, self.w["tp"])
+        return [self.send(v, v, d) for d in devs]
+    def after_z(self):
+        w = self.w
+        for c in self.cz: c.wait_recv()
+        devs = [w["a"], w["b"]] + ([w["peer"]] if self.peer else [])
+        self.c1 = self._fan(w["q"], devs)
+    def after_a(self):
+        w = self.w
+        self.c1[0].wait_recv()
+        self.c2 = self._fan(w["qa"], [w["b"]] + ([w["peer"]] if self.peer else []))
+    def after_b(self):
+        w = self.w
+        self.c1[1].wait_recv(); self.c2[0].wait_recv()
+        self.c3 = []
+        if self.peer:
+            self.c3 = self._fan(w["qb"], [w["peer"]]) + self._fan(w["qab"], [w["peer"]])
+    def finish(self):
+        if self.peer:
+            self.c1[2].wait_recv(); self.c2[1].wait_recv()
+            for c in self.c3: c.wait_recv()
+
+N_COPIES = 64
+
+def k12_kernel(len_ref, tok, wq, wos, vpk, e24, e96, rsel, fc1s, fc2s,
+               afull, qkv, wown, o_out, lse_ref, vec, mid, wo_h, fc1_h, fc2_h,
+               xp, vbuf, sb, rb, woc, o_loc, fq, fk, q2, m_s, l_s, acc, ss, rs, ls, *, B, pairs, stage=9):
+    w = place()
+    tp = w["tp"]
+    rows, D = tok.shape
+    W = pairs * 128
+    send = Sender(ss, rs)
+    first = tp == 0
+    sb[...] = jnp.zeros_like(sb)
+    pick = lambda c0, n: (jnp.where(first, wq[:, c0:c0 + W], wq[:, c0 + W:c0 + 2 * W]).astype(bf16),
+                          jnp.where(first, wq[:, c0 + W:c0 + 2 * W], wq[:, c0:c0 + W]).astype(bf16))
+    mine = []
+    for k in range(3):
+        own, oth = pick(k * D, W)
+        mine.append(own); sb[0:24, k * W:(k + 1) * W] = oth
+    own_o = jnp.where(first, wos[:, :W], wos[:, W:])
+    sb[0:24, 3 * W:4 * W] = jnp.where(first, wos[:, W:], wos[:, :W])
+    vbuf[w["z"], w["q"], tp] = vpk[...]
+    loc = [pltpu.make_async_copy(fc1s, fc1_h.at[w["z"], w["q"], tp], ls.at[0]),
+           pltpu.make_async_copy(fc2s, fc2_h.at[w["z"], w["q"], tp], ls.at[1])]
+    for c in loc: c.start()
+    enter(w)
+    cpre = send(sb, rb, w["peer"])
+    gv = Gather(send, w, vbuf.at[w["z"], w["q"], tp], lambda z, q, t: vbuf.at[z, q, t], lambda q, t: vbuf.at[:, q, t], True)
+    gv.start()
+    cx = send(tok, xp, w["peer"])
+    cpre.wait_recv()
+    other = rb[0:24, :].astype(f32)
+    me = jnp.concatenate(mine + [own_o], axis=1).astype(f32)
+    both = jnp.concatenate([jnp.where(first, me, other), jnp.where(first, other, me)], axis=0).astype(bf16)
+    wown[w["z"], w["q"]] = both[:, :3 * W]
+    woc[...] = both[:, 3 * W:]
+    gq = Gather(send, w, wown.at[w["z"], w["q"]], lambda z, q, t: wown.at[z, q], lambda q, t: wown.at[:, q], False)
+    gq.start()
+    cols = pl.ds(pl.multiple_of(tp * W, 128), W)
+    lw = pltpu.make_async_copy(woc, wo_h.at[w["z"], w["q"], :, cols], ls.at[2])
+    lw.start()
+    gv.after_z(); gv.after_a(); gv.after_b(); gv.finish()
+    small = nn(rsel[...], vbuf[...].reshape(512, 128)).astype(bf16)
+    dev = lax.broadcasted_iota(jnp.int32, (32, 1), 0)
+    lane = lax.broadcasted_iota(jnp.int32, (1, D), 1)
+    hit = (lane >= dev * 24) & (lane < dev * 24 + 24)
+    for v in range(6):
+        vec[v:v + 1, :] = colsum(jnp.where(hit, nn(small[v * 32:(v + 1) * 32], e24[...]), 0.0))
+    vec[6:8, :] = jnp.zeros((2, D), f32)
+    lane = lax.broadcasted_iota(jnp.int32, (1, 4 * D), 1)
+    hit = (lane >= dev * 96) & (lane < dev * 96 + 96)
+    for v in range(2):
+        mid[v:v + 1, :] = colsum(jnp.where(hit, nn(small[(6 + v) * 32:(7 + v) * 32], e96[...]), 0.0))
+    mid[2:8, :] = jnp.zeros((6, 4 * D), f32)
+    gq.after_z()
+    for c in loc: c.wait()
+    lw.wait()
+    go = Gather(send, w, woc, lambda z, q, t: wo_h.at[z, q, :, cols], lambda q, t: wo_h.at[:, q, :, cols], True)
+    g1 = Gather(send, w, fc1s, lambda z, q, t: fc1_h.at[z, q, t], lambda q, t: fc1_h.at[:, q, t], True)
+    g2 = Gather(send, w, fc2s, lambda z, q, t: fc2_h.at[z, q, t], lambda q, t: fc2_h.at[:, q, t], True)
+    go.start(); g1.start()
+    def normed(src, base):
+        def body(r, _):
+            sl = pl.ds(pl.multiple_of(r * 256, 256), 256)
+            xh, _r = stats(src[sl, :].astype(f32))
+            afull[pl.ds(pl.multiple_of(base + r * 256, 256), 256), :] = (xh * vec[0:1, :] + vec[1:2, :]).astype(bf16)
+            return 0
+        lax.fori_loop(0, rows // 256, body, 0)
+    normed(tok, tp * rows)
+    gq.after_a()
+    cx.wait_recv()
+    normed(xp, (1 - tp) * rows)
+    doc_features(len_ref, 2 * rows, fq, fk)
+    gq.after_b()
+    wfull = lambda: wown[...].reshape(D, 3 * W)
+    def proj(r, _):
+        sl = pl.ds(pl.multiple_of(r * 512, 512), 512)
+        qkv[sl, :] = nn(afull[sl, :], wfull()).astype(bf16)
+        return 0
+    lax.fori_loop(0, 2 * rows // 512, proj, 0)
+    nb = 2 * rows // B
+    half = lax.broadcasted_iota(jnp.int32, (1, 128), 1) < 64
+    causal = lax.broadcasted_iota(jnp.int32, (B, B), 0) <= lax.broadcasted_iota(jnp.int32, (B, B), 1)
+    causal = jnp.concatenate([causal, causal], axis=1)
+    def unit(u, _):
+        p, i = u // nb, u % nb
+        qs = pl.ds(pl.multiple_of(i * B, B), B)
+        lanes = lambda k: pl.ds(pl.multiple_of(k * W + p * 128, 128), 128)
+        q = qkv[qs, lanes(0)] * bf16(0.125)
+        fqb = fq[qs, :]
+        z = jnp.zeros_like(q)
+        q2[...] = jnp.concatenate([
+            jnp.concatenate([jnp.where(half, q, z), fqb], axis=1),
+            jnp.concatenate([jnp.where(half, z, q), fqb], axis=1)], axis=0)
+        def block(j, diag):
+            ks = pl.ds(pl.multiple_of(j * B, B), B)
+            s = nt(jnp.concatenate([qkv[ks, lanes(1)], fk[ks, :]], axis=1), q2[...])
+            if diag: s = jnp.where(causal, s, -BIG)
+            mn = jnp.max(s, axis=0, keepdims=True)
+            if not diag:
+                mo = m_s[...]
+                mn = jnp.maximum(mo, mn); al = jnp.exp(mo - mn)
+            e = jnp.exp(s - mn)
+            su = jnp.sum(e, axis=0, keepdims=True)
+            pv = tn(qkv[ks, lanes(2)], e.astype(bf16))
+            if diag: l_s[...] = su; acc[...] = pv
+            else: l_s[...] = l_s[...] * al + su; acc[...] = acc[...] * al + pv
+            m_s[...] = mn
+        block(i, True)
+        def kstep(j, _):
+            block(j, False); return 0
+        lax.fori_loop(0, i, kstep, 0)
+        l = l_s[...]
+        a = acc[...] * (1.0 / l)
+        ot = jnp.concatenate([a[:64, :B], a[64:, B:]], axis=0)
+        o_loc[qs, pl.ds(pl.multiple_of(p * 128, 128), 128)] = ot.T.astype(bf16)
+        lse = m_s[...] + jnp.log(l)
+        lse_ref[p, 0:1, qs] = lse[:, :B]
+        lse_ref[p, 1:2, qs] = lse[:, B:]
+        return 0
+    def units(lo, hi):
+        lax.fori_loop(lo, hi, unit, 0)
+    co = []
+    def share(p):
+        src = o_loc.at[pl.ds(pl.multiple_of((1 - tp) * rows, rows), rows), p * 128:(p + 1) * 128]
+        co.append(send(src, o_out.at[:, pl.ds(pl.multiple_of(tp * W + p * 128, 128), 128)], w["peer"]))
+    go.after_z(); g1.after_z(); g2.start()
+    units(0, 3)
+    go.after_a(); g1.after_a()
+    units(3, 4); share(0)
+    units(4, 6)
+    go.after_b(); g1.after_b(); g2.after_z()
+    units(6, 8); share(1)
+    g2.after_a()
+    units(8, 11)
+    g2.after_b()
+    units(11, 12); share(2)
+    o_out[:, cols] = o_loc[pl.ds(pl.multiple_of(tp * rows, rows), rows), :]
+    for c in co: c.wait_recv()
+    go.finish(); g1.finish(); g2.finish()
+    for c in send.all: c.wait_send()
+
+def consts_np(D):
+    k = np.arange(128)[:, None]
+    e24 = (np.arange(D)[None] % 24 == k).astype(np.float32)
+    e96 = (np.arange(4 * D)[None] % 96 == k).astype(np.float32)
+    r = np.arange(256)[:, None]
+    rsel = (np.arange(512)[None] == (r % 32) * 16 + r // 32).astype(np.float32)
+    return e24, e96, rsel
+
+def consts(D):
+    return [jnp.asarray(c, bf16) for c in consts_np(D)]
+
+def k12(lengths, tok, wq, wos, vpk, fc1s, fc2s, B=512):
+    rows, D = tok.shape
+    W = D // 2; pairs = W // 128
+    V, A = pl.BlockSpec(memory_space=pltpu.VMEM), pl.BlockSpec(memory_space=pl.ANY)
+    sds = jax.ShapeDtypeStruct
+    hid = fc1s.shape[0]
+    return pl.pallas_call(functools.partial(k12_kernel, B=B, pairs=pairs), name="forward",
+        out_shape=(sds((2 * rows, D), bf16), sds((2 * rows, 3 * W), bf16), sds((4, 4, 48, 3 * W), bf16), sds((rows, D), bf16),
+                   sds((pairs, 2, 2 * rows), f32), sds((8, D), f32), sds((8, 4 * D), f32),
+                   sds((4, 4, 48, D), bf16), sds((4, 4, 2, hid, D), bf16), sds((4, 4, 2, hid, D), bf16)),
+        in_specs=[pl.BlockSpec(memory_space=pltpu.SMEM)] + [V] * 7 + [A] * 2,
+        out_specs=(V,) * 7 + (A,) * 3,
+        scratch_shapes=[pltpu.VMEM((rows, D), bf16), pltpu.VMEM((4, 4, 2, 16, 128), bf16), pltpu.VMEM((32, 4 * W), bf16), pltpu.VMEM((32, 4 * W), bf16),
+                        pltpu.VMEM((48, W), bf16), pltpu.VMEM((2 * rows, W), bf16), pltpu.VMEM((2 * rows, 128), bf16), pltpu.VMEM((2 * rows, 128), bf16),
+                        pltpu.VMEM((2 * B, 256), bf16), pltpu.VMEM((1, 2 * B), f32), pltpu.VMEM((1, 2 * B), f32), pltpu.VMEM((128, 2 * B), f32),
+                        pltpu.SemaphoreType.DMA((N_COPIES,)), pltpu.SemaphoreType.DMA((N_COPIES,)), pltpu.SemaphoreType.DMA((3,))],
+        compiler_params=pltpu.CompilerParams(vmem_limit_bytes=60 << 20, collective_id=0, has_side_effects=True))(
+            lengths, tok, wq, wos, vpk, *consts(D), fc1s, fc2s)
+
+def pack_vectors(six, two):
+    n6 = jnp.pad(jnp.stack(six), ((0, 0), (0, 128 - six[0].shape[0])))
+    n2 = jnp.pad(jnp.stack(two), ((0, 8), (0, 128 - two[0].shape[0])))
+    return jnp.concatenate([n6, n2], axis=0)
+
+
+class Copy:
+    def __init__(self, ss, rs):
+        self.ss, self.rs, self.n, self.all = ss, rs, 0, []
+    def __call__(self, src, dst, dev):
+        c = pltpu.make_async_remote_copy(src_ref=src, dst_ref=dst, send_sem=self.ss.at[self.n], recv_sem=self.rs.at[self.n],
+                                         device_id=dev, device_id_type=MESH)
+        self.n += 1
+        self.all.append(c)
+        return c
+
+def add(x, y):
+    return (x.astype(f32) + y.astype(f32)).astype(x.dtype)
+
+class Scatter:
+    def __init__(self, copy, w, s, bb, ab, zb):
+        self.w, self.s, self.bb, self.ab, self.zb = w, s, bb, ab, zb
+        self.b = [copy(s.at[:, w["qb"]], bb.at[0], w["b"]), copy(s.at[:, w["qab"]], bb.at[1], w["b"])]
+        self.a = [copy(s.at[:, w["qa"]], ab, w["a"])]
+        self.z = [copy(s.at[w["zi"][k], w["q"]], zb.at[k], w["zs"][k]) for k in range(3)]
+    def go(self, cs):
+        for c in cs: c.start()
+    def start(self):
+        self.go(self.b)
+    def after_b(self):
+        for c in self.b: c.wait_recv()
+        for z in range(4):
+            self.s[z, self.w["qa"]] = add(self.s[z, self.w["qa"]], self.bb[1, z])
+        self.go(self.a)
+        for z in range(4):
+            self.s[z, self.w["q"]] = add(self.s[z, self.w["q"]], self.bb[0, z])
+    def after_a(self):
+        for c in self.a: c.wait_recv()
+        for z in range(4):
+            self.s[z, self.w["q"]] = add(self.s[z, self.w["q"]], self.ab[z])
+        self.go(self.z)
+    def result(self):
+        for c in self.z: c.wait_recv()
+        r = self.s[self.w["z"], self.w["q"]].astype(f32)
+        for k in range(3): r = r + self.zb[k].astype(f32)
+        return r
+
+def k45_kernel(len_ref, afull, wown, do, delta, lse_ref, vec, gvec, gmid, gwo, e24t, e96t, qkv_h, tok_h, dy_h, g1_h, g2_h,
+               gtok, gq_o, gwo_o, g1_o, g2_o, small_o,
+               qkv, tok, dy, do_own, dl_own, fq, fk, q2, do2, dq, dk, dv,
+               s1, r1, b1, a1, z1, s2, r2, b2, a2, z2, so, ro, bo, ao, zo, sq, bq, aq, zq,
+               sm, pm, s4, bm, am, zm, da, dsend, drecv, fo, xo, fqk, xq, ss, rs, ls, *, B, pairs):
+    w = place()
+    tp = w["tp"]
+    rows, D = tok.shape
+    W = pairs * 128
+    nb = 2 * rows // B
+    first = tp == 0
+    other = 1 - tp
+    mine_rows = pl.ds(pl.multiple_of(tp * rows, rows), rows)
+    mine_cols = pl.ds(pl.multiple_of(tp * W, 128), W)
+    other_cols = pl.ds(pl.multiple_of(other * W, 128), W)
+    copy = Copy(ss, rs)
+    c_do = copy(do.at[:, other_cols], do_own.at[mine_rows, :], w["peer"])
+    c_dl = copy(delta.at[pl.ds(pl.multiple_of(other * 8, 8), 8), :], dl_own.at[:, mine_rows], w["peer"])
+    c_r2 = copy(g2_h.at[:, :, other], r2, w["peer"])
+    c_r1 = copy(g1_h.at[:, :, other], r1, w["peer"])
+    c_ro = copy(gwo.at[:, other_cols], ro, w["peer"])
+    f1, f2 = Scatter(copy, w, s1, b1, a1, z1), Scatter(copy, w, s2, b2, a2, z2)
+    fo_ = Scatter(copy, w, so, bo, ao, zo)
+    fqs = [Scatter(copy, w, sq.at[p], bq.at[p], aq.at[p], zq.at[p]) for p in range(pairs)]
+    fm = Scatter(copy, w, s4, bm, am, zm)
+    c_pm = copy(sm.at[:, :, other], pm, w["peer"])
+    hr = rows // 2
+    c_da = [copy(dsend.at[pl.ds(k * hr, hr), :], drecv.at[pl.ds(k * hr, hr), :], w["peer"]) for k in range(2)]
+    n = gq_o.shape[0]
+    other_n = pl.ds(pl.multiple_of(other * n, 8), n)
+    mine_n = pl.ds(pl.multiple_of(tp * n, 8), n)
+    c_xo = copy(fo.at[other_n, :], xo, w["peer"])
+    c_xq = copy(fqk.at[other_n, :], xq, w["peer"])
+    l_q = pltpu.make_async_copy(qkv_h, qkv, ls.at[0])
+    l_2 = pltpu.make_async_copy(g2_h.at[:, :, tp], s2, ls.at[1])
+    l_1 = pltpu.make_async_copy(g1_h.at[:, :, tp], s1, ls.at[2])
+    l_t = pltpu.make_async_copy(tok_h, tok, ls.at[3])
+    l_y = pltpu.make_async_copy(dy_h, dy, ls.at[4])
+    for l in (l_q, l_2, l_1, l_t, l_y): l.start()
+    enter(w)
+    for c in (c_do, c_dl, c_ro, c_r2, c_r1): c.start()
+    do_own[mine_rows, :] = do[:, mine_cols]
+    dl_own[:, mine_rows] = delta[pl.ds(pl.multiple_of(tp * 8, 8), 8), :]
+    doc_features(len_ref, 2 * rows, fq, fk)
+    dev = lax.broadcasted_iota(jnp.int32, (32, 1, 1), 0)
+    def pieces(v, e, n):
+        lane = lax.broadcasted_iota(jnp.int32, (1, 1, v.shape[1]), 2)
+        hit = (lane >= dev * n) & (lane < dev * n + n)
+        t = jnp.where(hit, v[None], 0.0).reshape(256, v.shape[1])
+        hi = t.astype(bf16)
+        return nn(hi, e) + nn((t - hi.astype(f32)).astype(bf16), e)
+    early = pieces(gmid[...], e96t[...], 4 * D // 32) + pieces(gvec[...], e24t[...], D // 32)
+    sm[...] = early.reshape(4, 4, 2, 8, 128)
+    l_q.wait()
+    c_do.wait_recv(); c_dl.wait_recv()
+
+    half = lax.broadcasted_iota(jnp.int32, (1, 128), 1) < 64
+    causal = lax.broadcasted_iota(jnp.int32, (B, B), 0) <= lax.broadcasted_iota(jnp.int32, (B, B), 1)
+    causal = jnp.concatenate([causal, causal], axis=1)
+    def unit(u, _):
+        p, j = u // nb, u % nb
+        lanes = lambda k: pl.ds(pl.multiple_of(k * W + p * 128, 128), 128)
+        def at(k):
+            def deco(f): pl.when(u == k)(f)
+            return deco
+        @at(1)
+        def _():
+            c_r2.wait_recv(); l_2.wait()
+            for z in range(4):
+                for k in range(4): s2[z, k] = add(s2[z, k], r2[z, k])
+            f2.start()
+            c_ro.wait_recv()
+            so[...] = add(gwo[:, mine_cols], ro[...]).reshape(so.shape)
+            fo_.start()
+        @at(2)
+        def _():
+            c_r1.wait_recv(); l_1.wait()
+            for z in range(4):
+                for k in range(4): s1[z, k] = add(s1[z, k], r1[z, k])
+            f1.start()
+        @at(4)
+        def _():
+            f2.after_b(); fo_.after_b(); fqs[0].start()
+        @at(5)
+        def _():
+            f2.after_a(); fo_.after_a()
+        @at(6)
+        def _():
+            f1.after_b(); fqs[0].after_b()
+        @at(7)
+        def _():
+            fqs[0].after_a()
+        @at(8)
+        def _():
+            f1.after_a(); fqs[1].start()
+            g2_o[...] = f2.result()
+            fo[...] = fo_.result()
+            c_xo.start()
+        @at(9)
+        def _():
+            fqs[1].after_b()
+        @at(10)
+        def _():
+            fqs[1].after_a()
+        @pl.when(j == 0)
+        def _():
+            def prep(i, _):
+                qs = pl.ds(pl.multiple_of(i * B, B), B)
+                q = qkv[qs, lanes(0)] * bf16(0.125)
+                d = do_own[qs, pl.ds(pl.multiple_of(p * 128, 128), 128)]
+                fqb = fq[qs, :]
+                z = jnp.zeros_like(q)
+                q2[i] = jnp.concatenate([
+                    jnp.concatenate([jnp.where(half, q, z), fqb], axis=1),
+                    jnp.concatenate([jnp.where(half, z, q), fqb], axis=1)], axis=0)
+                do2[i] = jnp.concatenate([jnp.where(half, d, z), jnp.where(half, z, d)], axis=0)
+                dq[i] = jnp.zeros(dq.shape[1:], f32)
+                return 0
+            lax.fori_loop(0, nb, prep, 0)
+        ks = pl.ds(pl.multiple_of(j * B, B), B)
+        kt = qkv[ks, lanes(1)]
+        v = qkv[ks, lanes(2)]
+        k2 = jnp.concatenate([kt, fk[ks, :]], axis=1)
+        def block(i, diag):
+            qs = pl.ds(pl.multiple_of(i * B, B), B)
+            lse = jnp.concatenate([lse_ref[p, 0:1, qs], lse_ref[p, 1:2, qs]], axis=1)
+            d0 = pl.ds(2 * p, 1); d1 = pl.ds(2 * p + 1, 1)
+            dl = jnp.concatenate([dl_own[d0, qs], dl_own[d1, qs]], axis=1)
+            qq = q2[i]; dd = do2[i]
+            pt = jnp.exp(nt(k2, qq) - lse)
+            if diag: pt = jnp.where(causal, pt, 0.0)
+            ds = (pt * (nt(v, dd) - dl)).astype(bf16)
+            dvp = nn(pt.astype(bf16), dd)
+            dkp = nn(ds, qq[:, :128])
+            if diag: dv[...] = dvp; dk[...] = dkp
+            else: dv[...] += dvp; dk[...] += dkp
+            dq[i] += tn(ds, kt)
+        block(j, True)
+        def qstep(i, _):
+            block(i, False); return 0
+        lax.fori_loop(j + 1, nb, qstep, 0)
+        qkv[ks, lanes(1)] = dk[...].astype(bf16)
+        qkv[ks, lanes(2)] = dv[...].astype(bf16)
+        @pl.when(j == nb - 1)
+        def _():
+            def fin(i, _):
+                qs = pl.ds(pl.multiple_of(i * B, B), B)
+                d = dq[i]
+                qkv[qs, lanes(0)] = (jnp.where(half, d[:B], d[B:]) * 0.125).astype(bf16)
+                return 0
+            lax.fori_loop(0, nb, fin, 0)
+            g = jnp.concatenate([qkv[:, lanes(k)] for k in range(3)], axis=1)
+            sq[p] = tn(afull[...], g).astype(bf16).reshape(sq.shape[1:])
+        return 0
+    lax.fori_loop(0, pairs * nb, unit, 0)
+    fqs[2].start()
+    for k in range(2):
+        sl = pl.ds(pl.multiple_of(other * rows + k * hr, hr), hr)
+        dsend[k * hr:(k + 1) * hr, :] = nt(qkv[sl, :], wown[...]).astype(bf16)
+        c_da[k].start()
+    fqs[2].after_b()
+    g1_o[...] = f1.result()
+    for k in range(2):
+        sl = pl.ds(pl.multiple_of(tp * rows + k * hr, hr), hr)
+        da[k * hr:(k + 1) * hr, :] = nt(qkv[sl, :], wown[...])
+        if k == 0: fqs[2].after_a()
+    l_t.wait(); l_y.wait()
+    for c in c_da: c.wait_recv()
+    gain = vec[0:1, :]
+    def fin(r, st):
+        gg, gb = st
+        sl = pl.ds(pl.multiple_of(r * 256, 256), 256)
+        d = da[sl, :] + drecv[sl, :].astype(f32)
+        xh, xr = stats(tok[sl, :].astype(f32))
+        gtok[sl, :] = (dy[sl, :].astype(f32) + ln_back(d, xh, xr, gain)).astype(bf16)
+        return gg + colsum(d * xh), gb + colsum(d)
+    z = jnp.zeros((1, D), f32)
+    gg, gb = lax.fori_loop(0, rows // 256, fin, (z, z))
+    late = pieces(jnp.concatenate([gg, gb, jnp.zeros((6, D), f32)], axis=0), e24t[...], D // 32)
+    sm[...] = sm[...] + late.reshape(4, 4, 2, 8, 128)
+    c_pm.start()
+    for p in range(pairs):
+        fqk[:, p * 384:(p + 1) * 384] = fqs[p].result()
+    c_xq.start()
+    c_pm.wait_recv()
+    for z in range(4):
+        for k in range(4): s4[z, k] = sm[z, k, tp] + pm[z, k]
+    fm.start()
+    c_xo.wait_recv()
+    mine = fo[mine_n, :]
+    gwo_o[:, :W] = jnp.where(first, mine, xo[...])
+    gwo_o[:, W:] = jnp.where(first, xo[...], mine)
+    fm.after_b()
+    c_xq.wait_recv()
+    for p in range(pairs):
+        for k in range(3):
+            src = p * 384 + k * 128
+            mine = fqk[mine_n, src:src + 128]
+            oth = xq[:, src:src + 128]
+            c0 = k * D + p * 128
+            gq_o[:, c0:c0 + 128] = jnp.where(first, mine, oth)
+            gq_o[:, c0 + W:c0 + W + 128] = jnp.where(first, oth, mine)
+    fm.after_a()
+    small_o[...] = fm.result()
+    for c in copy.all: c.wait_send()
+
+def k45(lengths, afull, wown, do, delta, lse, vec, gvec, gmid, gwo, qkv, tok, dy, g1, g2, B=512):
+    rows, D = tok.shape
+    W = D // 2; pairs = W // 128; nb = 2 * rows // B
+    V, A = pl.BlockSpec(memory_space=pltpu.VMEM), pl.BlockSpec(memory_space=pl.ANY)
+    sds = jax.ShapeDtypeStruct
+    hid = g1.shape[3]
+    M = pltpu.VMEM
+    e24t, e96t = [c.T for c in consts_np(D)[:2]]
+    def flow(r, c, t, lead=()):
+        return [M(lead + (4, 4, r, c), t), M(lead + (2, 4, r, c), t), M(lead + (4, r, c), t), M(lead + (3, r, c), t)]
+    fc = flow(hid, D, bf16)
+    fc = [fc[0], M((4, 4, hid, D), bf16)] + fc[1:]
+    wo = flow(48, W, bf16)
+    wo = [wo[0], M((D, W), bf16)] + wo[1:]
+    sm = flow(8, 128, f32)
+    return pl.pallas_call(functools.partial(k45_kernel, B=B, pairs=pairs), name="backward",
+        out_shape=(sds((rows, D), bf16), sds((D // 32, 3 * D), f32), sds((D // 32, D), f32), sds((hid, D), f32), sds((hid, D), f32), sds((8, 128), f32)),
+        in_specs=[pl.BlockSpec(memory_space=pltpu.SMEM)] + [V] * 11 + [A] * 5,
+        out_specs=(V,) * 6,
+        scratch_shapes=[M((2 * rows, 3 * W), bf16), M((rows, D), bf16), M((rows, D), dy.dtype), M((2 * rows, W), bf16), M((8, 2 * rows), f32),
+                        M((2 * rows, 128), bf16), M((2 * rows, 128), bf16), M((nb, 2 * B, 256), bf16), M((nb, 2 * B, 128), bf16), M((nb, 2 * B, 128), f32),
+                        M((B, 128), f32), M((B, 128), f32)] + fc + fc + wo + flow(48, W, bf16, (pairs,)) +
+                       [M((4, 4, 2, 8, 128), f32), M((4, 4, 8, 128), f32)] + sm +
+                       [M((rows, D), f32), M((rows, D), bf16), M((rows, D), bf16), M((48, W), f32), M((24, W), f32), M((48, 3 * W), f32), M((24, 3 * W), f32),
+                        pltpu.SemaphoreType.DMA((64,)), pltpu.SemaphoreType.DMA((64,)), pltpu.SemaphoreType.DMA((5,))],
+        compiler_params=pltpu.CompilerParams(vmem_limit_bytes=63 << 20, collective_id=1, has_side_effects=True))(
+            lengths, afull, wown, do, delta, lse, vec, gvec, gmid, gwo, jnp.asarray(e24t, bf16), jnp.asarray(e96t, bf16), qkv, tok, dy, g1, g2)
+
+def local_fast(tokens, cotangent, lengths, qkv_weight, out_weight, pre_gain, pre_shift, sub_gain, sub_shift,
+          ffn_gain, ffn_shift, fc1_weight, mid_gain, mid_shift, fc2_weight):
+    rows, D = tokens.shape
+    vpk = pack_vectors([pre_gain, pre_shift, sub_gain, sub_shift, ffn_gain, ffn_shift], [mid_gain, mid_shift])
+    afull, qkv, wown, o, lse, vec, mid, wo, fc1, fc2 = k12(lengths, tokens, qkv_weight, out_weight, vpk, fc1_weight, fc2_weight)
+    block_out, dy, do, delta, gwo, g1, g2, gvec, gmid = ffn(o, tokens, cotangent, wo.reshape(D, D), fc1.reshape(4 * D, D), fc2.reshape(4 * D, D), vec, mid)
+    shape = (4, 4, 2, fc1_weight.shape[0], D)
+    gtok, gq, gwo, g1, g2, small = k45(lengths, afull, wown.reshape(D, -1), do, delta, lse, vec, gvec, gmid, gwo, qkv, tokens, dy, g1.reshape(shape), g2.reshape(shape))
+    n, m = pre_gain.shape[0], mid_gain.shape[0]
+    return (block_out, gtok, gq, gwo, small[0, :n], small[1, :n], small[2, :n], small[3, :n], small[4, :n], small[5, :n],
+            g1, small[6, :m], small[7, :m], g2)
 
 def norm(v):
     return stats(v)
 
 
-def local(tokens, cotangent, lengths, qkv_weight, out_weight, pre_gain, pre_shift, sub_gain, sub_shift,
+def local_any(tokens, cotangent, lengths, qkv_weight, out_weight, pre_gain, pre_shift, sub_gain, sub_shift,
           ffn_gain, ffn_shift, fc1_weight, mid_gain, mid_shift, fc2_weight):
     rows, D = tokens.shape
     W = D // 2
@@ -351,25 +877,31 @@
     qkv = nn(afull, wown).astype(bf16)
     o_own, lse = attn_fwd(lengths, qkv, B=512)
     o = lax.all_to_all(o_own, "tp", 0, 1, tiled=True)
-    vec = jnp.concatenate([small[2:6], jnp.zeros((4, D), f32)], axis=0)
-    block_out, dy, do, delta, gwo, gfc1, gfc2, gvec, gmg, gmb = ffn(o, tokens, cotangent, wo, fc1, fc2, vec, mid[0], mid[1])
+    vec = jnp.concatenate([small, jnp.zeros((2, D), f32)], axis=0)
+    block_out, dy, do, delta, gwo, gfc1, gfc2, gvec, gmid = ffn(
+        o, tokens, cotangent, wo, fc1, fc2, vec, jnp.concatenate([mid, jnp.zeros((6, 4 * D), f32)], axis=0))
     do_own = lax.all_to_all(do, "tp", 1, 0, tiled=True)
     dl_own = lax.all_to_all(delta, "tp", 0, 1, tiled=True)
     dqkv = attn_bwd(lengths, qkv, do_own, lse, dl_own, B=512)
     gq = tn(afull, dqkv)
     da = lax.psum_scatter(nt(dqkv, wown), "tp", scatter_dimension=0, tiled=True)
-    grad_tokens = (dy + ln_back(da, xh, xr, small[0])).astype(bf16)
+    grad_tokens = (dy.astype(f32) + ln_back(da, xh, xr, small[0])).astype(bf16)
     scatter = lambda v: lax.psum_scatter(v, both, scatter_dimension=0, tiled=True)
     gq = lax.psum_scatter(gq, "dp", scatter_dimension=0, tiled=True)
     n = gq.shape[0] // 2
     gq = lax.all_to_all(gq.reshape(2, n, 3, 1, W), "tp", 0, 3, tiled=True).reshape(n, 3 * D)
-    small_grads = scatter(jnp.concatenate([jnp.stack([colsum(da * xh)[0], colsum(da)[0]]), gvec[:4]], axis=0).T).T
-    mid_grads = scatter(jnp.stack([gmg.reshape(-1), gmb.reshape(-1)], axis=1)).T
+    small_grads = scatter(jnp.concatenate([jnp.stack([colsum(da * xh)[0], colsum(da)[0]]), gvec[2:6]], axis=0).T).T
+    mid_grads = scatter(gmid[6:8].T).T
     gwo = scatter(gwo.astype(f32))
     gfc1 = scatter(gfc1.reshape(-1, D).astype(f32))
     gfc2 = scatter(gfc2.reshape(-1, D).astype(f32))
     return (block_out, grad_tokens, gq, gwo, small_grads[0], small_grads[1], small_grads[2], small_grads[3],
             small_grads[4], small_grads[5], gfc1, mid_grads[0], mid_grads[1], gfc2)
+
+
+def local(*arrays):
+    fits = lax.axis_size("dp") == 16 and lax.axis_size("tp") == 2
+    return (local_fast if fits else local_any)(*arrays)
 
 
 def solution(mesh):

time: 1030 us -> 319 us (0.31)
  waiting for transfers between devices: 614 us -> 0 us
  blocking collectives: 136 us -> 0 us
  Pallas kernels: 179 us -> 308 us
  other arithmetic: 27.2 us -> 1.28 us
  matrix products: 25.6 us -> 0 us
  between operations: 14.4 us -> 0.7 us
  local copies, waits for them, and re-layouts: 21.4 us -> 8.95 us
    reduce_scatter x5 -> x0, waiting for transfers between devices: 488 us -> none  [the longest x3 341 us: local(): lax.psum_scatter(v, both, scatter_dimension=0, tiled=True)]
    pallas_call x2, Pallas kernels: 92.5 us -> 221 us  [the longest x1 119 us: k45(): pl.pallas_call(functools.partial(k45_kernel, B=B, pairs=pairs), name='bac...]
    all_gather x5 -> x0, waiting for transfers between devices: 119 us -> none  [the longest x4 119 us: local(): gather = lambda a: lax.all_gather(a, both, axis=0, tiled=True)]
    all_gather x2 -> x0, blocking collectives: 80.5 us -> none  [local(): gather = lambda a: lax.all_gather(a, both, axis=0, tiled=True)]
    unnamed x1 -> x0, blocking collectives: 40.7 us -> none
    dot_general x3 -> x0, matrix products: 25.6 us -> none  [the longest x1 8.86 us: nn(): lax.dot_general(a, b, (((1,), (0,)), ((), ())), preferred_element_type=f32)]
    convert_element_type x6 -> x0, other arithmetic: 21.8 us -> none  [the longest x1 6.73 us: local(): gfc2 = scatter(gfc2.reshape(-1, D).astype(f32))]
    all_to_all x3 -> x0, blocking collectives: 14.9 us -> none  [the longest x1 6.31 us: local(): o = lax.all_to_all(o_own, 'tp', 0, 1, tiled=True)]
  transfers between devices with their start and end apart: 12 -> 0, of which waited for: 9 -> 0; matrix products, arithmetic and copies ran while one was open for 7% -> 0% of each run, Pallas kernels for 9% -> 0%
where the time goes in v2:
time: 319 us; the launch traced here: 318 us
  Pallas kernels  308 us (97%)
  local copies, waits for them, and re-layouts  8.95 us (3%)
    pallas_call x1, Pallas kernels, k45(): pl.pallas_call(functools.partial(k45_kernel, B=B, pairs=pairs), name='bac...  119 us
    pallas_call x1, Pallas kernels, k12(): pl.pallas_call(functools.partial(k12_kernel, B=B, pairs=pairs), name='for...  102 us
    pallas_call x1, Pallas kernels, ffn(): pl.pallas_call(functools.partial(ffn_kernel, T=T, NT=NT, NC=NC), name='ff...  86.4 us

profile of v2, /device:TPU:0, one launch (start us, length us, event | category | flops | bytes accessed | tf_op | source)
XLA Modules:
  0.0 318.5 jit_solution(8652246314093779840)
XLA Ops:
  0.6 0.8 stack.36
  1.4 0.7 fusion.6
  2.1 0.6 fusion.7.vpk
  2.7 101.7 %forward.1 = (bf16[2048,768]{1,0:T(8,128)(2,1)}, bf16[2048,1152]{1,0:T(8,128)(2,1)}, bf16[4,4,48,1152]{3,2,1,0:T(8,128)(2,1)}, bf16[1024,768]{1,0:T(8,128)(2,1)}...) custom-call(s32[1,8]{1,0:T(1,128)} %len_ref.3, ...), custom_call_target="tpu_custom_call" | custom-call | tf_op jit(solution)/shard_map/forward/pallas_call | solution.py:551
  104.4 86.4 %ffn.1 = (bf16[1024,768]{1,0:T(8,128)(2,1)}, bf16[1024,768]{1,0:T(8,128)(2,1)}, bf16[1024,768]{1,0:T(8,128)(2,1)}, f32[16,1024]{1,0:T(8,128)}, bf16[768,768]{1,0...) custom-call(bf16[1024,768]{1,0:T(8,128)(2,1)} %get-tuple-element.39., ...), custom_call_target="tpu_custom_call" | custom-call | tf_op jit(solution)/shard_map/ffn/pallas_call | solution.py:312
  190.8 119.4 %backward.1 = (bf16[1024,768]{1,0:T(8,128)(2,1)}, f32[24,2304]{1,0:T(8,128)}, f32[24,768]{1,0:T(8,128)}, f32[96,768]{1,0:T(8,128)}, f32[96,768]{1,0:T(8,128)}, /*index=5*/f32[8,128]{1,0:T(8,128)}) custom-call(s32[1,8]{1,0:T(1,128)} %len_ref.3, bf16[2048,768]{1,0:T(8,128)(2,1)} %get-tuple-element.46.afull, bf16[768,1152]{1,0:T(8,128)(2,1)} %bitcast.34, ...), custom_call_target="tpu_custom_call" | custom-call | tf_op jit(solution)/shard_map/backward/pallas_call | solution.py:832
  310.3 1.3 slice_bitcast_fusion
  311.5 1.4 slice_bitcast_fusion.2
  313.0 0.0 copy-start.2
  313.0 0.0 copy-start.3
  313.0 0.0 copy-start.1
  313.0 0.0 copy-start
  313.0 2.7 copy.40
  315.7 0.0 copy-done.2
  315.7 0.7 copy.41
  316.4 0.0 copy-done.3
  316.4 0.6 copy.42
  317.1 0.0 copy-done.1
  317.1 0.7 copy.43
  317.8 0.0 copy-done
  317.8 0.7 copy.44
Async XLA Ops:
  313.0 2.8 copy-start.2
  313.0 3.4 %copy-start.3 = (f32[24,768]{1,0:T(8,128)S(1)}, f32[24,768]{1,0:T(8,128)}, u32[]{:S(2)}) copy-start(f32[24,768]{1,0:T(8,128)} %get-tuple-element.89) | copy-start | bytes 221188
  313.0 4.1 %copy-start.1 = (f32[96,768]{1,0:T(8,128)S(1)}, f32[96,768]{1,0:T(8,128)}, u32[]{:S(2)}) copy-start(f32[96,768]{1,0:T(8,128)} %get-tuple-element.96) | copy-start | bytes 884740
  313.0 4.8 %copy-start = (f32[96,768]{1,0:T(8,128)S(1)}, f32[96,768]{1,0:T(8,128)}, u32[]{:S(2)}) copy-start(f32[96,768]{1,0:T(8,128)} %get-tuple-element.99) | copy-start | bytes 884740
